TPU v7x, 256 devices: a whole 4x4x8 slice. The times are simulated.
256 devices in a mesh: blk: 64 (over x, z_hi, y, core), rep: 4 (over z_lo).
Axes of the slice: x: 4, y: 4, z: 8 (z_hi: 2, z_lo: 4; z = z_hi * 4 + z_lo), core: 2. Of those that a mesh axis runs over, the one named last changes fastest.
Arguments:
- src_points: bfloat16 [131072, 256], P(('blk', 'rep')), may hold values from -0.75 to 0.75
- src_log_mass: float32 [131072], P(('blk', 'rep')), may hold values from -3 to 3
- tgt_points: bfloat16 [65536, 256], P('blk'), may hold values from -0.75 to 0.75
- tgt_log_mass: float32 [65536], P('blk'), may hold values from -3 to 3
- initial_potential: float32 [65536], P('blk'), may hold values from -61 to 61
- pair_list: int32 [64, 7], replicated, may hold values from -1 to 63, as said below
- pair_count: int32 [64], replicated, may hold values from 1 to 7, as said below
Outputs:
- source_potential: float32 [131072], P(('blk', 'rep'))
- target_potential: float32 [65536], P('blk')
Inputs may be any that keep to these rules, and one draw needn't show every extreme that they name: Row s of pair_list lists the target blocks kept by source block s: entry 0 is s itself, the next pair_count[s] - 1 entries are distinct blocks (s + o) mod 64 with 1 <= |o| <= 3, and the remaining entries are -1. `pair_count`: some block has 7 kept target blocks and some other block has 1.
All inputs are finite; a program needn't handle non-finite values.
Results may differ from a plain program's by a relative error of at most 0.0003.
Values may be sent and summed in bfloat16 or wider, within the bound.
No kernel may reach another device: no remote copies, remote signals or barrier semaphores. Data moves between devices by JAX's collectives and lax.ppermute only.
A program may use at most 64 MiB of HBM per device.

v0:
```python
import jax
import jax.numpy as jnp
from jax import lax
from jax.sharding import PartitionSpec as P

REACH = 3
ITERS = 2


EPS_START = 0.5
NEG_FILL = -1e30


def shifted_2(value, axis, steps):
    count = lax.axis_size(axis)
    pairs = [(source, (source + steps) % count) for source in range(count)]
    return lax.ppermute(value, axis, pairs)


def merged(part, axis, combine):
    gathered = jax.tree.map(lambda a: lax.all_gather(a, axis), part)

    def take(source):
        return jax.tree.map(lambda a: lax.dynamic_index_in_dim(a, source, 0, False), gathered)

    return lax.fori_loop(
        1, lax.axis_size(axis), lambda source, state: combine(state, take(source)), take(0)
    )


def half_norms(points):
    widened = points.astype(jnp.float32)
    return 0.5 * jnp.sum(widened * widened, axis=1)


def scaled_cost(src, src_half, tgt, tgt_half, inv_eps):
    cross = lax.dot_general(src, tgt, (((1,), (1,)), ((), ())), preferred_element_type=jnp.float32)
    return (src_half[:, None] + tgt_half[None, :] - cross) * inv_eps


def join_partials(first_top, first_total, second_top, second_total):
    top = jnp.maximum(first_top, second_top)
    return (top, first_total * jnp.exp(first_top - top) + second_total * jnp.exp(second_top - top))


def combine_parts(first, second):
    return join_partials(first[0], first[1], second[0], second[1])


def block_kept(pair_list, pair_count, source_block, target_block):
    row_ids = pair_list[source_block]
    in_use = jnp.arange(row_ids.shape[0], dtype=jnp.int32) < pair_count[source_block]
    return jnp.any((row_ids == target_block) & in_use)


def tour_targets(message, visit_block, running):
    my_block = lax.axis_index("blk")
    cycle_size = lax.axis_size("blk")
    message = shifted_2(message, "blk", -REACH)

    def cycle_step(turn_index, carry_pair):
        running, message = carry_pair
        held_block = (my_block + REACH - turn_index) % cycle_size
        running, message = visit_block(running, message, held_block)
        message = shifted_2(message, "blk", 1)
        return (running, message)

    running, message = lax.fori_loop(0, 2 * REACH, cycle_step, (running, message))
    running, message = visit_block(running, message, (my_block - REACH) % cycle_size)
    return (running, (message,))


def local(
    src_points, src_log_mass, tgt_points, tgt_log_mass, initial_potential, pair_list, pair_count
):
    my_block = lax.axis_index("blk")
    src_half = half_norms(src_points)
    rows = src_points.shape[0]
    columns = tgt_points.shape[0]
    target_pot = initial_potential
    source_pot = jnp.zeros((rows,), jnp.float32)
    for sweep_index in range(ITERS):
        epsilon = EPS_START * 0.5**sweep_index
        inv_eps = 1.0 / epsilon
        shifted = tgt_log_mass + target_pot * inv_eps
        row_start = (jnp.full((rows,), NEG_FILL, jnp.float32), jnp.zeros((rows,), jnp.float32))
        column_start = (
            jnp.full((columns,), NEG_FILL, jnp.float32),
            jnp.zeros((columns,), jnp.float32),
        )

        def row_visit(running, message, held_block):
            tgt_block, tgt_shifted = message

            def row_update(partials):
                cost = scaled_cost(src_points, src_half, tgt_block, half_norms(tgt_block), inv_eps)
                scores = tgt_shifted[None, :] - cost
                top = jnp.max(scores, axis=1)
                total = jnp.sum(jnp.exp(scores - top[:, None]), axis=1)
                return join_partials(partials[0], partials[1], top, total)

            kept = block_kept(pair_list, pair_count, my_block, held_block)
            running = lax.cond(kept, row_update, lambda partials: partials, running)
            return (running, message)

        row_parts, unused = tour_targets((tgt_points, shifted), row_visit, row_start)
        source_pot = -epsilon * (row_parts[0] + jnp.log(row_parts[1]))
        weighted = src_log_mass + source_pot * inv_eps

        def column_visit(running, message, held_block):
            tgt_block, top, total = message

            def column_update(partials):
                cost = scaled_cost(src_points, src_half, tgt_block, half_norms(tgt_block), inv_eps)
                scores = weighted[:, None] - cost
                col_top = jnp.max(scores, axis=0)
                col_total = jnp.sum(jnp.exp(scores - col_top[None, :]), axis=0)
                return join_partials(partials[0], partials[1], col_top, col_total)

            kept = block_kept(pair_list, pair_count, my_block, held_block)
            top, total = lax.cond(kept, column_update, lambda partials: partials, (top, total))
            return (running, (tgt_block, top, total))

        dummy = jnp.zeros((), jnp.float32)
        unused, travelled = tour_targets(
            (tgt_points, column_start[0], column_start[1]), column_visit, dummy
        )
        col_top, col_total = shifted_2((travelled[0][1], travelled[0][2]), "blk", -REACH)
        merged_top, merged_total = merged((col_top, col_total), "rep", combine_parts)
        target_pot = -epsilon * (merged_top + jnp.log(merged_total))
    return (source_pot, target_pot)


def solution(mesh):
    in_specs = (
        P(("blk", "rep"), None),
        P(("blk", "rep")),
        P("blk", None),
        P("blk"),
        P("blk"),
        P(),
        P(),
    )
    out_specs = (P(("blk", "rep")), P("blk"))
    return jax.shard_map(local, mesh=mesh, in_specs=in_specs, out_specs=out_specs, check_vma=False)
```

profile of v0, /device:TPU:1, one launch (start us, length us, event | category | flops | bytes accessed | tf_op | source)
XLA Modules:
  0.0 584.2 jit_solution(14468355463403160145)
XLA Ops:
  0.6 13.0 %collective-permute-start.10 = (bf16[1024,256]{1,0:T(8,128)(2,1)}, bf16[1024,256]{1,0:T(8,128)(2,1)S(1)}, u32[]{:S(2)}, u32[]{:S(2)}) collective-permute-start(bf16[1024,256]{1,0:T(8,128)(2,1)} %param.37), channel_id=1, source_target_pairs={{0,244},{4,248},{8,252},{12,0},{16,4},{20,8},{24,12},{28,16},{32,2... | collective-permute-start | bytes 1572872 | tf_op jit(solution)/shard_map/ppermute | solution.py:17
  16.8 1.3 dynamic_slice.138
  19.2 1.3 fusion.6
  21.1 15.9 %collective-permute-done.11 = f32[1024]{0:T(1024)S(1)} collective-permute-done((f32[1024]{0:T(1024)S(1)}, f32[1024]{0:T(1024)S(1)}, u32[]{:S(2)}, u32[]{:S(2)}) %collective-permute-start.11) | collective-permute-done | bytes 4128 | tf_op jit(solution)/shard_map/ppermute | solution.py:17
  37.7 93.8 %while.122 = (s32[]{:T(128)}, f32[512]{0:T(512)S(1)}, f32[512]{0:T(512)S(1)}, bf16[1024,256]{1,0:T(8,128)(2,1)S(1)}, f32[1024]{0:T(1024)S(1)}, /*index=5*/s32[]{...) while((s32[]{:T(128)}, f32[512]{0:T(512)S(1)}, ...), condition=%wide.region_9.10_spmd, body=%wide.region_2.9_spmd.sunk | while | flops 272893984 | bytes 8716752 | solution.py:68
  41.0 3.9 collective-permute-done.1
  45.7 2.4 collective-permute-start
  50.7 9.6 %collective-permute-done.1 = f32[1024]{0:T(1024)S(1)} collective-permute-done((f32[1024]{0:T(1024)}, f32[1024]{0:T(1024)S(1)}, u32[]{:S(2)}, u32[]{:S(2)}) %collective-permute-start.1) | collective-permute-done | bytes 4128 | tf_op jit(solution)/shard_map/while/body/eval_jaxpr/ppermute | solution.py:17
  63.6 3.6 conditional.16
  64.9 1.7 fusion.7
  67.2 10.9 %collective-permute-done.1 = f32[1024]{0:T(1024)S(1)} collective-permute-done((f32[1024]{0:T(1024)}, f32[1024]{0:T(1024)S(1)}, u32[]{:S(2)}, u32[]{:S(2)}) %collective-permute-start.1) | collective-permute-done | bytes 4128 | tf_op jit(solution)/shard_map/while/body/eval_jaxpr/ppermute | solution.py:17
  81.4 3.6 conditional.16
  82.7 1.7 fusion.7
  85.0 10.9 %collective-permute-done.1 = f32[1024]{0:T(1024)S(1)} collective-permute-done((f32[1024]{0:T(1024)}, f32[1024]{0:T(1024)S(1)}, u32[]{:S(2)}, u32[]{:S(2)}) %collective-permute-start.1) | collective-permute-done | bytes 4128 | tf_op jit(solution)/shard_map/while/body/eval_jaxpr/ppermute | solution.py:17
  99.2 14.5 %collective-permute-done.1 = f32[1024]{0:T(1024)S(1)} collective-permute-done((f32[1024]{0:T(1024)}, f32[1024]{0:T(1024)S(1)}, u32[]{:S(2)}, u32[]{:S(2)}) %collective-permute-start.1) | collective-permute-done | bytes 4128 | tf_op jit(solution)/shard_map/while/body/eval_jaxpr/ppermute | solution.py:17
  117.0 14.5 %collective-permute-done.1 = f32[1024]{0:T(1024)S(1)} collective-permute-done((f32[1024]{0:T(1024)}, f32[1024]{0:T(1024)S(1)}, u32[]{:S(2)}, u32[]{:S(2)}) %collective-permute-start.1) | collective-permute-done | bytes 4128 | tf_op jit(solution)/shard_map/while/body/eval_jaxpr/ppermute | solution.py:17
  132.2 108.2 %while.123 = (s32[]{:T(128)}, bf16[1024,256]{1,0:T(8,128)(2,1)S(1)}, f32[1024]{0:T(1024)S(1)}, f32[1024]{0:T(1024)S(1)}, s32[]{:T(128)}, /*index=5*/s32[1,7]{1,0...) while((s32[]{:T(128)}, bf16[1024,256]{1,0:T(8,128)(2,1)S(1)}, ...), condition=%wide.region_22.23_spmd, body=%wide.region_15.22_spmd.sunk | while | flops 272896032 | bytes 8757752 | solution.py:68
  135.1 15.9 %collective-permute-done.3 = f32[1024]{0:T(1024)S(1)} collective-permute-done((f32[1024]{0:T(1024)S(1)}, f32[1024]{0:T(1024)S(1)}, u32[]{:S(2)}, u32[]{:S(2)}) %collective-permute-start.3) | collective-permute-done | bytes 4128 | tf_op jit(solution)/shard_map/while/body/eval_jaxpr/ppermute | solution.py:17
  154.1 14.8 %collective-permute-done.3 = f32[1024]{0:T(1024)S(1)} collective-permute-done((f32[1024]{0:T(1024)S(1)}, f32[1024]{0:T(1024)S(1)}, u32[]{:S(2)}, u32[]{:S(2)}) %collective-permute-start.3) | collective-permute-done | bytes 4128 | tf_op jit(solution)/shard_map/while/body/eval_jaxpr/ppermute | solution.py:17
  171.7 3.3 conditional.17
  173.0 1.7 fusion.9
  175.2 11.5 %collective-permute-done.3 = f32[1024]{0:T(1024)S(1)} collective-permute-done((f32[1024]{0:T(1024)S(1)}, f32[1024]{0:T(1024)S(1)}, u32[]{:S(2)}, u32[]{:S(2)}) %collective-permute-start.3) | collective-permute-done | bytes 4128 | tf_op jit(solution)/shard_map/while/body/eval_jaxpr/ppermute | solution.py:17
  189.5 3.3 conditional.17
  190.8 1.7 fusion.9
  193.1 14.8 %collective-permute-done.3 = f32[1024]{0:T(1024)S(1)} collective-permute-done((f32[1024]{0:T(1024)S(1)}, f32[1024]{0:T(1024)S(1)}, u32[]{:S(2)}, u32[]{:S(2)}) %collective-permute-start.3) | collective-permute-done | bytes 4128 | tf_op jit(solution)/shard_map/while/body/eval_jaxpr/ppermute | solution.py:17
  210.9 11.5 %collective-permute-done.3 = f32[1024]{0:T(1024)S(1)} collective-permute-done((f32[1024]{0:T(1024)S(1)}, f32[1024]{0:T(1024)S(1)}, u32[]{:S(2)}, u32[]{:S(2)}) %collective-permute-start.3) | collective-permute-done | bytes 4128 | tf_op jit(solution)/shard_map/while/body/eval_jaxpr/ppermute | solution.py:17
  225.4 14.9 %collective-permute-done.3 = f32[1024]{0:T(1024)S(1)} collective-permute-done((f32[1024]{0:T(1024)S(1)}, f32[1024]{0:T(1024)S(1)}, u32[]{:S(2)}, u32[]{:S(2)}) %collective-permute-start.3) | collective-permute-done | bytes 4128 | tf_op jit(solution)/shard_map/while/body/eval_jaxpr/ppermute | solution.py:17
  240.6 15.6 %collective-permute-start.14 = (f32[1024]{0:T(1024)S(1)}, f32[1024]{0:T(1024)S(1)}, u32[]{:S(2)}, u32[]{:S(2)}) collective-permute-start(f32[1024]{0:T(1024)S(1)} %get-tuple-element.1915), channel_id=1, source_target_pairs={{0,244},{4,248},{8,252},{12,0},{16,4},{20,8},{24,12},{28,16},{32,2... | collective-permute-start | bytes 12296 | tf_op jit(solution)/shard_map/ppermute | solution.py:17
  256.9 35.2 %all-gather = f32[4096]{0:T(1024)S(1)} all-gather(f32[1024]{0:T(1024)S(1)} %collective-permute-done.14), channel_id=2, replica_groups=mesh['blk'=64,'rep'=4] {'rep'}, dimensions={0}, use_global_device_ids=true | all-gather | bytes 20480 | tf_op jit(solution)/shard_map/all_gather | solution.py:21
  292.1 10.2 %all-gather.1 = f32[4096]{0:T(1024)S(1)} all-gather(f32[1024]{0:T(1024)S(1)} %collective-permute-done.15), channel_id=3, replica_groups=mesh['blk'=64,'rep'=4] {'rep'}, dimensions={0}, use_global_device_ids=true | all-gather | bytes 20480 | tf_op jit(solution)/shard_map/all_gather | solution.py:21
  302.6 16.0 %collective-permute-start.16 = (f32[1024]{0:T(1024)S(1)}, f32[1024]{0:T(1024)S(1)}, u32[]{:S(2)}, u32[]{:S(2)}) collective-permute-start(f32[1024]{0:T(1024)S(1)} %multiply_add_fusion.10), channel_id=1, source_target_pairs={{0,244},{4,248},{8,252},{12,0},{16,4},{20,8},{24,12},{28,16},{32,2... | collective-permute-start | bytes 12296 | tf_op jit(solution)/shard_map/ppermute | solution.py:17
  319.3 93.9 %while.125 = (s32[]{:T(128)}, f32[512]{0:T(512)S(1)}, f32[512]{0:T(512)S(1)}, bf16[1024,256]{1,0:T(8,128)(2,1)S(1)}, f32[1024]{0:T(1024)S(1)}, /*index=5*/s32[]{...) while((s32[]{:T(128)}, f32[512]{0:T(512)S(1)}, ...), condition=%wide.region_37.38_spmd, body=%wide.region_30.37_spmd.sunk | while | flops 272893984 | bytes 8716752 | solution.py:68
  320.7 1.3 fusion.37
  322.7 3.8 collective-permute-done.6
  327.3 2.4 collective-permute-start.5
  330.3 1.3 fusion.37
  332.4 3.8 collective-permute-done.6
  337.0 2.4 collective-permute-start.5
  340.0 1.3 fusion.37
  342.0 3.6 conditional.18
  343.3 1.7 fusion.11
  345.6 8.5 %collective-permute-done.6 = f32[1024]{0:T(1024)S(1)} collective-permute-done((f32[1024]{0:T(1024)}, f32[1024]{0:T(1024)S(1)}, u32[]{:S(2)}, u32[]{:S(2)}) %collective-permute-start.6) | collective-permute-done | bytes 4128 | tf_op jit(solution)/shard_map/while/body/eval_jaxpr/ppermute | solution.py:17
  355.5 1.3 fusion.37
  357.5 3.6 conditional.18
  358.8 1.7 fusion.11
  361.0 10.8 %collective-permute-done.6 = f32[1024]{0:T(1024)S(1)} collective-permute-done((f32[1024]{0:T(1024)}, f32[1024]{0:T(1024)S(1)}, u32[]{:S(2)}, u32[]{:S(2)}) %collective-permute-start.6) | collective-permute-done | bytes 4128 | tf_op jit(solution)/shard_map/while/body/eval_jaxpr/ppermute | solution.py:17
  373.2 1.3 fusion.37
  375.3 14.4 %collective-permute-done.6 = f32[1024]{0:T(1024)S(1)} collective-permute-done((f32[1024]{0:T(1024)}, f32[1024]{0:T(1024)S(1)}, u32[]{:S(2)}, u32[]{:S(2)}) %collective-permute-start.6) | collective-permute-done | bytes 4128 | tf_op jit(solution)/shard_map/while/body/eval_jaxpr/ppermute | solution.py:17
  391.0 1.3 fusion.37
  393.1 20.1 %collective-permute-done.6 = f32[1024]{0:T(1024)S(1)} collective-permute-done((f32[1024]{0:T(1024)}, f32[1024]{0:T(1024)S(1)}, u32[]{:S(2)}, u32[]{:S(2)}) %collective-permute-start.6) | collective-permute-done | bytes 4128 | tf_op jit(solution)/shard_map/while/body/eval_jaxpr/ppermute | solution.py:17
  413.9 127.0 %while.126 = (s32[]{:T(128)}, bf16[1024,256]{1,0:T(8,128)(2,1)S(1)}, f32[1024]{0:T(1024)S(1)}, f32[1024]{0:T(1024)S(1)}, s32[]{:T(128)}, /*index=5*/s32[1,7]{1,0...) while((s32[]{:T(128)}, bf16[1024,256]{1,0:T(8,128)(2,1)S(1)}, ...), condition=%wide.region_50.51_spmd, body=%wide.region_43.50_spmd.sunk | while | flops 272896032 | bytes 8757752 | solution.py:68
  416.8 20.2 %collective-permute-done.8 = f32[1024]{0:T(1024)S(1)} collective-permute-done((f32[1024]{0:T(1024)S(1)}, f32[1024]{0:T(1024)S(1)}, u32[]{:S(2)}, u32[]{:S(2)}) %collective-permute-start.8) | collective-permute-done | bytes 4128 | tf_op jit(solution)/shard_map/while/body/eval_jaxpr/ppermute | solution.py:17
  440.0 14.9 %collective-permute-done.8 = f32[1024]{0:T(1024)S(1)} collective-permute-done((f32[1024]{0:T(1024)S(1)}, f32[1024]{0:T(1024)S(1)}, u32[]{:S(2)}, u32[]{:S(2)}) %collective-permute-start.8) | collective-permute-done | bytes 4128 | tf_op jit(solution)/shard_map/while/body/eval_jaxpr/ppermute | solution.py:17
  457.7 3.3 conditional.19
  459.0 1.7 fusion.13
  461.2 11.5 %collective-permute-done.8 = f32[1024]{0:T(1024)S(1)} collective-permute-done((f32[1024]{0:T(1024)S(1)}, f32[1024]{0:T(1024)S(1)}, u32[]{:S(2)}, u32[]{:S(2)}) %collective-permute-start.8) | collective-permute-done | bytes 4128 | tf_op jit(solution)/shard_map/while/body/eval_jaxpr/ppermute | solution.py:17
  475.5 3.3 conditional.19
  476.8 1.7 fusion.13
  479.0 20.6 %collective-permute-done.8 = f32[1024]{0:T(1024)S(1)} collective-permute-done((f32[1024]{0:T(1024)S(1)}, f32[1024]{0:T(1024)S(1)}, u32[]{:S(2)}, u32[]{:S(2)}) %collective-permute-start.8) | collective-permute-done | bytes 4128 | tf_op jit(solution)/shard_map/while/body/eval_jaxpr/ppermute | solution.py:17
  502.6 17.2 %collective-permute-done.8 = f32[1024]{0:T(1024)S(1)} collective-permute-done((f32[1024]{0:T(1024)S(1)}, f32[1024]{0:T(1024)S(1)}, u32[]{:S(2)}, u32[]{:S(2)}) %collective-permute-start.8) | collective-permute-done | bytes 4128 | tf_op jit(solution)/shard_map/while/body/eval_jaxpr/ppermute | solution.py:17
  522.8 18.0 %collective-permute-done.8 = f32[1024]{0:T(1024)S(1)} collective-permute-done((f32[1024]{0:T(1024)S(1)}, f32[1024]{0:T(1024)S(1)}, u32[]{:S(2)}, u32[]{:S(2)}) %collective-permute-start.8) | collective-permute-done | bytes 4128 | tf_op jit(solution)/shard_map/while/body/eval_jaxpr/ppermute | solution.py:17
  541.1 15.4 %collective-permute-start.17 = (f32[1024]{0:T(1024)S(1)}, f32[1024]{0:T(1024)S(1)}, u32[]{:S(2)}, u32[]{:S(2)}) collective-permute-start(f32[1024]{0:T(1024)S(1)} %get-tuple-element.1928), channel_id=1, source_target_pairs={{0,244},{4,248},{8,252},{12,0},{16,4},{20,8},{24,12},{28,16},{32,2... | collective-permute-start | bytes 12296 | tf_op jit(solution)/shard_map/ppermute | solution.py:17
  557.2 15.9 %all-gather.2 = f32[4096]{0:T(1024)S(1)} all-gather(f32[1024]{0:T(1024)S(1)} %collective-permute-done.17), channel_id=4, replica_groups=mesh['blk'=64,'rep'=4] {'rep'}, dimensions={0}, use_global_device_ids=true | all-gather | bytes 20480 | tf_op jit(solution)/shard_map/all_gather | solution.py:21
  573.1 10.2 %all-gather.3 = f32[4096]{0:T(1024)S(1)} all-gather(f32[1024]{0:T(1024)S(1)} %collective-permute-done.18), channel_id=5, replica_groups=mesh['blk'=64,'rep'=4] {'rep'}, dimensions={0}, use_global_device_ids=true | all-gather | bytes 20480 | tf_op jit(solution)/shard_map/all_gather | solution.py:21
  (294 shorter events, 75.8 us)
Async XLA Ops:
  0.6 36.5 %collective-permute-start.10 = (bf16[1024,256]{1,0:T(8,128)(2,1)}, bf16[1024,256]{1,0:T(8,128)(2,1)S(1)}, u32[]{:S(2)}, u32[]{:S(2)}) collective-permute-start(bf16[1024,256]{1,0:T(8,128)(2,1)} %param.37), channel_id=1, source_target_pairs={{0,244},{4,248},{8,252},{12,0},{16,4},{20,8},{24,12},{28,16},{32,2... | collective-permute-start | bytes 1572872 | tf_op jit(solution)/shard_map/ppermute | solution.py:17
  14.4 22.8 %collective-permute-start.13 = (f32[1024]{0:T(1024)S(1)}, f32[1024]{0:T(1024)S(1)}, u32[]{:S(2)}, u32[]{:S(2)}) collective-permute-start(f32[1024]{0:T(1024)S(1)} %multiply_add_fusion.11), channel_id=1, source_target_pairs={{0,244},{4,248},{8,252},{12,0},{16,4},{20,8},{24,12},{28,16},{32,2... | collective-permute-start | bytes 12296 | tf_op jit(solution)/shard_map/ppermute | solution.py:17
  15.1 22.0 %collective-permute-start.11 = (f32[1024]{0:T(1024)S(1)}, f32[1024]{0:T(1024)S(1)}, u32[]{:S(2)}, u32[]{:S(2)}) collective-permute-start(f32[1024]{0:T(1024)S(1)} %broadcast.136), channel_id=1, source_target_pairs={{0,244},{4,248},{8,252},{12,0},{16,4},{20,8},{24,12},{28,16},{32,2... | collective-permute-start | bytes 12296 | tf_op jit(solution)/shard_map/ppermute | solution.py:17
  15.8 21.3 %collective-permute-start.12 = (f32[1024]{0:T(1024)S(1)}, f32[1024]{0:T(1024)S(1)}, u32[]{:S(2)}, u32[]{:S(2)}) collective-permute-start(f32[1024]{0:T(1024)S(1)} %broadcast.137), channel_id=1, source_target_pairs={{0,244},{4,248},{8,252},{12,0},{16,4},{20,8},{24,12},{28,16},{32,2... | collective-permute-start | bytes 12296 | tf_op jit(solution)/shard_map/ppermute | solution.py:17
  45.7 14.6 %collective-permute-start = (bf16[1024,256]{1,0:T(8,128)(2,1)}, bf16[1024,256]{1,0:T(8,128)(2,1)S(1)}, u32[]{:S(2)}, u32[]{:S(2)}) collective-permute-start(bf16[1024,256]{1,0:T(8,128)(2,1)} %copy.36), channel_id=1, source_target_pairs={{0,4},{4,8},{8,12},{12,16},{16,20},{20,24},{24,28},{28,32},{32,36}... | collective-permute-start | bytes 1572872 | tf_op jit(solution)/shard_map/while/body/eval_jaxpr/ppermute | solution.py:17
  48.7 11.6 %collective-permute-start.1 = (f32[1024]{0:T(1024)}, f32[1024]{0:T(1024)S(1)}, u32[]{:S(2)}, u32[]{:S(2)}) collective-permute-start(f32[1024]{0:T(1024)} %copy.37), channel_id=1, source_target_pairs={{0,4},{4,8},{8,12},{12,16},{16,20},{20,24},{24,28},{28,32},{32,36}... | collective-permute-start | bytes 12296 | tf_op jit(solution)/shard_map/while/body/eval_jaxpr/ppermute | solution.py:17
  61.1 17.0 %collective-permute-start = (bf16[1024,256]{1,0:T(8,128)(2,1)}, bf16[1024,256]{1,0:T(8,128)(2,1)S(1)}, u32[]{:S(2)}, u32[]{:S(2)}) collective-permute-start(bf16[1024,256]{1,0:T(8,128)(2,1)} %copy.36), channel_id=1, source_target_pairs={{0,4},{4,8},{8,12},{12,16},{16,20},{20,24},{24,28},{28,32},{32,36}... | collective-permute-start | bytes 1572872 | tf_op jit(solution)/shard_map/while/body/eval_jaxpr/ppermute | solution.py:17
  61.7 16.4 %collective-permute-start.1 = (f32[1024]{0:T(1024)}, f32[1024]{0:T(1024)S(1)}, u32[]{:S(2)}, u32[]{:S(2)}) collective-permute-start(f32[1024]{0:T(1024)} %copy.37), channel_id=1, source_target_pairs={{0,4},{4,8},{8,12},{12,16},{16,20},{20,24},{24,28},{28,32},{32,36}... | collective-permute-start | bytes 12296 | tf_op jit(solution)/shard_map/while/body/eval_jaxpr/ppermute | solution.py:17
  78.9 17.0 %collective-permute-start = (bf16[1024,256]{1,0:T(8,128)(2,1)}, bf16[1024,256]{1,0:T(8,128)(2,1)S(1)}, u32[]{:S(2)}, u32[]{:S(2)}) collective-permute-start(bf16[1024,256]{1,0:T(8,128)(2,1)} %copy.36), channel_id=1, source_target_pairs={{0,4},{4,8},{8,12},{12,16},{16,20},{20,24},{24,28},{28,32},{32,36}... | collective-permute-start | bytes 1572872 | tf_op jit(solution)/shard_map/while/body/eval_jaxpr/ppermute | solution.py:17
  79.5 16.4 %collective-permute-start.1 = (f32[1024]{0:T(1024)}, f32[1024]{0:T(1024)S(1)}, u32[]{:S(2)}, u32[]{:S(2)}) collective-permute-start(f32[1024]{0:T(1024)} %copy.37), channel_id=1, source_target_pairs={{0,4},{4,8},{8,12},{12,16},{16,20},{20,24},{24,28},{28,32},{32,36}... | collective-permute-start | bytes 12296 | tf_op jit(solution)/shard_map/while/body/eval_jaxpr/ppermute | solution.py:17
  96.7 17.0 %collective-permute-start = (bf16[1024,256]{1,0:T(8,128)(2,1)}, bf16[1024,256]{1,0:T(8,128)(2,1)S(1)}, u32[]{:S(2)}, u32[]{:S(2)}) collective-permute-start(bf16[1024,256]{1,0:T(8,128)(2,1)} %copy.36), channel_id=1, source_target_pairs={{0,4},{4,8},{8,12},{12,16},{16,20},{20,24},{24,28},{28,32},{32,36}... | collective-permute-start | bytes 1572872 | tf_op jit(solution)/shard_map/while/body/eval_jaxpr/ppermute | solution.py:17
  97.3 16.4 %collective-permute-start.1 = (f32[1024]{0:T(1024)}, f32[1024]{0:T(1024)S(1)}, u32[]{:S(2)}, u32[]{:S(2)}) collective-permute-start(f32[1024]{0:T(1024)} %copy.37), channel_id=1, source_target_pairs={{0,4},{4,8},{8,12},{12,16},{16,20},{20,24},{24,28},{28,32},{32,36}... | collective-permute-start | bytes 12296 | tf_op jit(solution)/shard_map/while/body/eval_jaxpr/ppermute | solution.py:17
  114.5 17.0 %collective-permute-start = (bf16[1024,256]{1,0:T(8,128)(2,1)}, bf16[1024,256]{1,0:T(8,128)(2,1)S(1)}, u32[]{:S(2)}, u32[]{:S(2)}) collective-permute-start(bf16[1024,256]{1,0:T(8,128)(2,1)} %copy.36), channel_id=1, source_target_pairs={{0,4},{4,8},{8,12},{12,16},{16,20},{20,24},{24,28},{28,32},{32,36}... | collective-permute-start | bytes 1572872 | tf_op jit(solution)/shard_map/while/body/eval_jaxpr/ppermute | solution.py:17
  115.1 16.4 %collective-permute-start.1 = (f32[1024]{0:T(1024)}, f32[1024]{0:T(1024)S(1)}, u32[]{:S(2)}, u32[]{:S(2)}) collective-permute-start(f32[1024]{0:T(1024)} %copy.37), channel_id=1, source_target_pairs={{0,4},{4,8},{8,12},{12,16},{16,20},{20,24},{24,28},{28,32},{32,36}... | collective-permute-start | bytes 12296 | tf_op jit(solution)/shard_map/while/body/eval_jaxpr/ppermute | solution.py:17
  133.0 18.1 %collective-permute-start.2 = (bf16[1024,256]{1,0:T(8,128)(2,1)}, bf16[1024,256]{1,0:T(8,128)(2,1)S(1)}, u32[]{:S(2)}, u32[]{:S(2)}) collective-permute-start(bf16[1024,256]{1,0:T(8,128)(2,1)} %copy.52), channel_id=1, source_target_pairs={{0,4},{4,8},{8,12},{12,16},{16,20},{20,24},{24,28},{28,32},{32,36}... | collective-permute-start | bytes 1572872 | tf_op jit(solution)/shard_map/while/body/eval_jaxpr/ppermute | solution.py:17
  135.0 16.1 %collective-permute-start.3 = (f32[1024]{0:T(1024)S(1)}, f32[1024]{0:T(1024)S(1)}, u32[]{:S(2)}, u32[]{:S(2)}) collective-permute-start(f32[1024]{0:T(1024)S(1)} %get-tuple-element.2378), channel_id=1, source_target_pairs={{0,4},{4,8},{8,12},{12,16},{16,20},{20,24},{24,28},{28,32},{32,36}... | collective-permute-start | bytes 12296 | tf_op jit(solution)/shard_map/while/body/eval_jaxpr/ppermute | solution.py:17
  135.1 16.1 %collective-permute-start.4 = (f32[1024]{0:T(1024)S(1)}, f32[1024]{0:T(1024)S(1)}, u32[]{:S(2)}, u32[]{:S(2)}) collective-permute-start(f32[1024]{0:T(1024)S(1)} %get-tuple-element.2379), channel_id=1, source_target_pairs={{0,4},{4,8},{8,12},{12,16},{16,20},{20,24},{24,28},{28,32},{32,36}... | collective-permute-start | bytes 12296 | tf_op jit(solution)/shard_map/while/body/eval_jaxpr/ppermute | solution.py:17
  152.0 17.0 %collective-permute-start.2 = (bf16[1024,256]{1,0:T(8,128)(2,1)}, bf16[1024,256]{1,0:T(8,128)(2,1)S(1)}, u32[]{:S(2)}, u32[]{:S(2)}) collective-permute-start(bf16[1024,256]{1,0:T(8,128)(2,1)} %copy.52), channel_id=1, source_target_pairs={{0,4},{4,8},{8,12},{12,16},{16,20},{20,24},{24,28},{28,32},{32,36}... | collective-permute-start | bytes 1572872 | tf_op jit(solution)/shard_map/while/body/eval_jaxpr/ppermute | solution.py:17
  153.9 15.0 %collective-permute-start.3 = (f32[1024]{0:T(1024)S(1)}, f32[1024]{0:T(1024)S(1)}, u32[]{:S(2)}, u32[]{:S(2)}) collective-permute-start(f32[1024]{0:T(1024)S(1)} %get-tuple-element.2378), channel_id=1, source_target_pairs={{0,4},{4,8},{8,12},{12,16},{16,20},{20,24},{24,28},{28,32},{32,36}... | collective-permute-start | bytes 12296 | tf_op jit(solution)/shard_map/while/body/eval_jaxpr/ppermute | solution.py:17
  154.0 15.0 %collective-permute-start.4 = (f32[1024]{0:T(1024)S(1)}, f32[1024]{0:T(1024)S(1)}, u32[]{:S(2)}, u32[]{:S(2)}) collective-permute-start(f32[1024]{0:T(1024)S(1)} %get-tuple-element.2379), channel_id=1, source_target_pairs={{0,4},{4,8},{8,12},{12,16},{16,20},{20,24},{24,28},{28,32},{32,36}... | collective-permute-start | bytes 12296 | tf_op jit(solution)/shard_map/while/body/eval_jaxpr/ppermute | solution.py:17
  169.8 17.0 %collective-permute-start.2 = (bf16[1024,256]{1,0:T(8,128)(2,1)}, bf16[1024,256]{1,0:T(8,128)(2,1)S(1)}, u32[]{:S(2)}, u32[]{:S(2)}) collective-permute-start(bf16[1024,256]{1,0:T(8,128)(2,1)} %copy.52), channel_id=1, source_target_pairs={{0,4},{4,8},{8,12},{12,16},{16,20},{20,24},{24,28},{28,32},{32,36}... | collective-permute-start | bytes 1572872 | tf_op jit(solution)/shard_map/while/body/eval_jaxpr/ppermute | solution.py:17
  175.0 11.7 %collective-permute-start.3 = (f32[1024]{0:T(1024)S(1)}, f32[1024]{0:T(1024)S(1)}, u32[]{:S(2)}, u32[]{:S(2)}) collective-permute-start(f32[1024]{0:T(1024)S(1)} %get-tuple-element.2378), channel_id=1, source_target_pairs={{0,4},{4,8},{8,12},{12,16},{16,20},{20,24},{24,28},{28,32},{32,36}... | collective-permute-start | bytes 12296 | tf_op jit(solution)/shard_map/while/body/eval_jaxpr/ppermute | solution.py:17
  175.1 11.7 %collective-permute-start.4 = (f32[1024]{0:T(1024)S(1)}, f32[1024]{0:T(1024)S(1)}, u32[]{:S(2)}, u32[]{:S(2)}) collective-permute-start(f32[1024]{0:T(1024)S(1)} %get-tuple-element.2379), channel_id=1, source_target_pairs={{0,4},{4,8},{8,12},{12,16},{16,20},{20,24},{24,28},{28,32},{32,36}... | collective-permute-start | bytes 12296 | tf_op jit(solution)/shard_map/while/body/eval_jaxpr/ppermute | solution.py:17
  187.6 20.4 %collective-permute-start.2 = (bf16[1024,256]{1,0:T(8,128)(2,1)}, bf16[1024,256]{1,0:T(8,128)(2,1)S(1)}, u32[]{:S(2)}, u32[]{:S(2)}) collective-permute-start(bf16[1024,256]{1,0:T(8,128)(2,1)} %copy.52), channel_id=1, source_target_pairs={{0,4},{4,8},{8,12},{12,16},{16,20},{20,24},{24,28},{28,32},{32,36}... | collective-permute-start | bytes 1572872 | tf_op jit(solution)/shard_map/while/body/eval_jaxpr/ppermute | solution.py:17
  192.9 15.0 %collective-permute-start.3 = (f32[1024]{0:T(1024)S(1)}, f32[1024]{0:T(1024)S(1)}, u32[]{:S(2)}, u32[]{:S(2)}) collective-permute-start(f32[1024]{0:T(1024)S(1)} %get-tuple-element.2378), channel_id=1, source_target_pairs={{0,4},{4,8},{8,12},{12,16},{16,20},{20,24},{24,28},{28,32},{32,36}... | collective-permute-start | bytes 12296 | tf_op jit(solution)/shard_map/while/body/eval_jaxpr/ppermute | solution.py:17
  193.0 15.0 %collective-permute-start.4 = (f32[1024]{0:T(1024)S(1)}, f32[1024]{0:T(1024)S(1)}, u32[]{:S(2)}, u32[]{:S(2)}) collective-permute-start(f32[1024]{0:T(1024)S(1)} %get-tuple-element.2379), channel_id=1, source_target_pairs={{0,4},{4,8},{8,12},{12,16},{16,20},{20,24},{24,28},{28,32},{32,36}... | collective-permute-start | bytes 12296 | tf_op jit(solution)/shard_map/while/body/eval_jaxpr/ppermute | solution.py:17
  208.8 13.7 %collective-permute-start.2 = (bf16[1024,256]{1,0:T(8,128)(2,1)}, bf16[1024,256]{1,0:T(8,128)(2,1)S(1)}, u32[]{:S(2)}, u32[]{:S(2)}) collective-permute-start(bf16[1024,256]{1,0:T(8,128)(2,1)} %copy.52), channel_id=1, source_target_pairs={{0,4},{4,8},{8,12},{12,16},{16,20},{20,24},{24,28},{28,32},{32,36}... | collective-permute-start | bytes 1572872 | tf_op jit(solution)/shard_map/while/body/eval_jaxpr/ppermute | solution.py:17
  210.7 11.7 %collective-permute-start.3 = (f32[1024]{0:T(1024)S(1)}, f32[1024]{0:T(1024)S(1)}, u32[]{:S(2)}, u32[]{:S(2)}) collective-permute-start(f32[1024]{0:T(1024)S(1)} %get-tuple-element.2378), channel_id=1, source_target_pairs={{0,4},{4,8},{8,12},{12,16},{16,20},{20,24},{24,28},{28,32},{32,36}... | collective-permute-start | bytes 12296 | tf_op jit(solution)/shard_map/while/body/eval_jaxpr/ppermute | solution.py:17
  210.8 11.7 %collective-permute-start.4 = (f32[1024]{0:T(1024)S(1)}, f32[1024]{0:T(1024)S(1)}, u32[]{:S(2)}, u32[]{:S(2)}) collective-permute-start(f32[1024]{0:T(1024)S(1)} %get-tuple-element.2379), channel_id=1, source_target_pairs={{0,4},{4,8},{8,12},{12,16},{16,20},{20,24},{24,28},{28,32},{32,36}... | collective-permute-start | bytes 12296 | tf_op jit(solution)/shard_map/while/body/eval_jaxpr/ppermute | solution.py:17
  223.3 17.1 %collective-permute-start.2 = (bf16[1024,256]{1,0:T(8,128)(2,1)}, bf16[1024,256]{1,0:T(8,128)(2,1)S(1)}, u32[]{:S(2)}, u32[]{:S(2)}) collective-permute-start(bf16[1024,256]{1,0:T(8,128)(2,1)} %copy.52), channel_id=1, source_target_pairs={{0,4},{4,8},{8,12},{12,16},{16,20},{20,24},{24,28},{28,32},{32,36}... | collective-permute-start | bytes 1572872 | tf_op jit(solution)/shard_map/while/body/eval_jaxpr/ppermute | solution.py:17
  225.2 15.1 %collective-permute-start.3 = (f32[1024]{0:T(1024)S(1)}, f32[1024]{0:T(1024)S(1)}, u32[]{:S(2)}, u32[]{:S(2)}) collective-permute-start(f32[1024]{0:T(1024)S(1)} %get-tuple-element.2378), channel_id=1, source_target_pairs={{0,4},{4,8},{8,12},{12,16},{16,20},{20,24},{24,28},{28,32},{32,36}... | collective-permute-start | bytes 12296 | tf_op jit(solution)/shard_map/while/body/eval_jaxpr/ppermute | solution.py:17
  225.3 15.1 %collective-permute-start.4 = (f32[1024]{0:T(1024)S(1)}, f32[1024]{0:T(1024)S(1)}, u32[]{:S(2)}, u32[]{:S(2)}) collective-permute-start(f32[1024]{0:T(1024)S(1)} %get-tuple-element.2379), channel_id=1, source_target_pairs={{0,4},{4,8},{8,12},{12,16},{16,20},{20,24},{24,28},{28,32},{32,36}... | collective-permute-start | bytes 12296 | tf_op jit(solution)/shard_map/while/body/eval_jaxpr/ppermute | solution.py:17
  240.6 16.3 %collective-permute-start.14 = (f32[1024]{0:T(1024)S(1)}, f32[1024]{0:T(1024)S(1)}, u32[]{:S(2)}, u32[]{:S(2)}) collective-permute-start(f32[1024]{0:T(1024)S(1)} %get-tuple-element.1915), channel_id=1, source_target_pairs={{0,244},{4,248},{8,252},{12,0},{16,4},{20,8},{24,12},{28,16},{32,2... | collective-permute-start | bytes 12296 | tf_op jit(solution)/shard_map/ppermute | solution.py:17
  256.1 35.9 %collective-permute-start.15 = (f32[1024]{0:T(1024)S(1)}, f32[1024]{0:T(1024)S(1)}, u32[]{:S(2)}, u32[]{:S(2)}) collective-permute-start(f32[1024]{0:T(1024)S(1)} %get-tuple-element.1916), channel_id=1, source_target_pairs={{0,244},{4,248},{8,252},{12,0},{16,4},{20,8},{24,12},{28,16},{32,2... | collective-permute-start | bytes 12296 | tf_op jit(solution)/shard_map/ppermute | solution.py:17
  302.6 16.7 %collective-permute-start.16 = (f32[1024]{0:T(1024)S(1)}, f32[1024]{0:T(1024)S(1)}, u32[]{:S(2)}, u32[]{:S(2)}) collective-permute-start(f32[1024]{0:T(1024)S(1)} %multiply_add_fusion.10), channel_id=1, source_target_pairs={{0,244},{4,248},{8,252},{12,0},{16,4},{20,8},{24,12},{28,16},{32,2... | collective-permute-start | bytes 12296 | tf_op jit(solution)/shard_map/ppermute | solution.py:17
  327.3 8.9 %collective-permute-start.5 = (bf16[1024,256]{1,0:T(8,128)(2,1)}, bf16[1024,256]{1,0:T(8,128)(2,1)S(1)}, u32[]{:S(2)}, u32[]{:S(2)}) collective-permute-start(bf16[1024,256]{1,0:T(8,128)(2,1)} %copy.80), channel_id=1, source_target_pairs={{0,4},{4,8},{8,12},{12,16},{16,20},{20,24},{24,28},{28,32},{32,36}... | collective-permute-start | bytes 1572872 | tf_op jit(solution)/shard_map/while/body/eval_jaxpr/ppermute | solution.py:17
  337.0 17.1 %collective-permute-start.5 = (bf16[1024,256]{1,0:T(8,128)(2,1)}, bf16[1024,256]{1,0:T(8,128)(2,1)S(1)}, u32[]{:S(2)}, u32[]{:S(2)}) collective-permute-start(bf16[1024,256]{1,0:T(8,128)(2,1)} %copy.80), channel_id=1, source_target_pairs={{0,4},{4,8},{8,12},{12,16},{16,20},{20,24},{24,28},{28,32},{32,36}... | collective-permute-start | bytes 1572872 | tf_op jit(solution)/shard_map/while/body/eval_jaxpr/ppermute | solution.py:17
  340.0 14.1 %collective-permute-start.6 = (f32[1024]{0:T(1024)}, f32[1024]{0:T(1024)S(1)}, u32[]{:S(2)}, u32[]{:S(2)}) collective-permute-start(f32[1024]{0:T(1024)} %copy.81), channel_id=1, source_target_pairs={{0,4},{4,8},{8,12},{12,16},{16,20},{20,24},{24,28},{28,32},{32,36}... | collective-permute-start | bytes 12296 | tf_op jit(solution)/shard_map/while/body/eval_jaxpr/ppermute | solution.py:17
  354.9 17.0 %collective-permute-start.5 = (bf16[1024,256]{1,0:T(8,128)(2,1)}, bf16[1024,256]{1,0:T(8,128)(2,1)S(1)}, u32[]{:S(2)}, u32[]{:S(2)}) collective-permute-start(bf16[1024,256]{1,0:T(8,128)(2,1)} %copy.80), channel_id=1, source_target_pairs={{0,4},{4,8},{8,12},{12,16},{16,20},{20,24},{24,28},{28,32},{32,36}... | collective-permute-start | bytes 1572872 | tf_op jit(solution)/shard_map/while/body/eval_jaxpr/ppermute | solution.py:17
  355.4 16.4 %collective-permute-start.6 = (f32[1024]{0:T(1024)}, f32[1024]{0:T(1024)S(1)}, u32[]{:S(2)}, u32[]{:S(2)}) collective-permute-start(f32[1024]{0:T(1024)} %copy.81), channel_id=1, source_target_pairs={{0,4},{4,8},{8,12},{12,16},{16,20},{20,24},{24,28},{28,32},{32,36}... | collective-permute-start | bytes 12296 | tf_op jit(solution)/shard_map/while/body/eval_jaxpr/ppermute | solution.py:17
  372.6 17.0 %collective-permute-start.5 = (bf16[1024,256]{1,0:T(8,128)(2,1)}, bf16[1024,256]{1,0:T(8,128)(2,1)S(1)}, u32[]{:S(2)}, u32[]{:S(2)}) collective-permute-start(bf16[1024,256]{1,0:T(8,128)(2,1)} %copy.80), channel_id=1, source_target_pairs={{0,4},{4,8},{8,12},{12,16},{16,20},{20,24},{24,28},{28,32},{32,36}... | collective-permute-start | bytes 1572872 | tf_op jit(solution)/shard_map/while/body/eval_jaxpr/ppermute | solution.py:17
  373.2 16.4 %collective-permute-start.6 = (f32[1024]{0:T(1024)}, f32[1024]{0:T(1024)S(1)}, u32[]{:S(2)}, u32[]{:S(2)}) collective-permute-start(f32[1024]{0:T(1024)} %copy.81), channel_id=1, source_target_pairs={{0,4},{4,8},{8,12},{12,16},{16,20},{20,24},{24,28},{28,32},{32,36}... | collective-permute-start | bytes 12296 | tf_op jit(solution)/shard_map/while/body/eval_jaxpr/ppermute | solution.py:17
  390.4 22.8 %collective-permute-start.5 = (bf16[1024,256]{1,0:T(8,128)(2,1)}, bf16[1024,256]{1,0:T(8,128)(2,1)S(1)}, u32[]{:S(2)}, u32[]{:S(2)}) collective-permute-start(bf16[1024,256]{1,0:T(8,128)(2,1)} %copy.80), channel_id=1, source_target_pairs={{0,4},{4,8},{8,12},{12,16},{16,20},{20,24},{24,28},{28,32},{32,36}... | collective-permute-start | bytes 1572872 | tf_op jit(solution)/shard_map/while/body/eval_jaxpr/ppermute | solution.py:17
  391.0 22.2 %collective-permute-start.6 = (f32[1024]{0:T(1024)}, f32[1024]{0:T(1024)S(1)}, u32[]{:S(2)}, u32[]{:S(2)}) collective-permute-start(f32[1024]{0:T(1024)} %copy.81), channel_id=1, source_target_pairs={{0,4},{4,8},{8,12},{12,16},{16,20},{20,24},{24,28},{28,32},{32,36}... | collective-permute-start | bytes 12296 | tf_op jit(solution)/shard_map/while/body/eval_jaxpr/ppermute | solution.py:17
  414.7 22.4 %collective-permute-start.7 = (bf16[1024,256]{1,0:T(8,128)(2,1)}, bf16[1024,256]{1,0:T(8,128)(2,1)S(1)}, u32[]{:S(2)}, u32[]{:S(2)}) collective-permute-start(bf16[1024,256]{1,0:T(8,128)(2,1)} %copy.96), channel_id=1, source_target_pairs={{0,4},{4,8},{8,12},{12,16},{16,20},{20,24},{24,28},{28,32},{32,36}... | collective-permute-start | bytes 1572872 | tf_op jit(solution)/shard_map/while/body/eval_jaxpr/ppermute | solution.py:17
  416.6 20.4 %collective-permute-start.8 = (f32[1024]{0:T(1024)S(1)}, f32[1024]{0:T(1024)S(1)}, u32[]{:S(2)}, u32[]{:S(2)}) collective-permute-start(f32[1024]{0:T(1024)S(1)} %get-tuple-element.2411), channel_id=1, source_target_pairs={{0,4},{4,8},{8,12},{12,16},{16,20},{20,24},{24,28},{28,32},{32,36}... | collective-permute-start | bytes 12296 | tf_op jit(solution)/shard_map/while/body/eval_jaxpr/ppermute | solution.py:17
  416.7 20.4 %collective-permute-start.9 = (f32[1024]{0:T(1024)S(1)}, f32[1024]{0:T(1024)S(1)}, u32[]{:S(2)}, u32[]{:S(2)}) collective-permute-start(f32[1024]{0:T(1024)S(1)} %get-tuple-element.2412), channel_id=1, source_target_pairs={{0,4},{4,8},{8,12},{12,16},{16,20},{20,24},{24,28},{28,32},{32,36}... | collective-permute-start | bytes 12296 | tf_op jit(solution)/shard_map/while/body/eval_jaxpr/ppermute | solution.py:17
  437.9 17.1 %collective-permute-start.7 = (bf16[1024,256]{1,0:T(8,128)(2,1)}, bf16[1024,256]{1,0:T(8,128)(2,1)S(1)}, u32[]{:S(2)}, u32[]{:S(2)}) collective-permute-start(bf16[1024,256]{1,0:T(8,128)(2,1)} %copy.96), channel_id=1, source_target_pairs={{0,4},{4,8},{8,12},{12,16},{16,20},{20,24},{24,28},{28,32},{32,36}... | collective-permute-start | bytes 1572872 | tf_op jit(solution)/shard_map/while/body/eval_jaxpr/ppermute | solution.py:17
  439.8 15.1 %collective-permute-start.8 = (f32[1024]{0:T(1024)S(1)}, f32[1024]{0:T(1024)S(1)}, u32[]{:S(2)}, u32[]{:S(2)}) collective-permute-start(f32[1024]{0:T(1024)S(1)} %get-tuple-element.2411), channel_id=1, source_target_pairs={{0,4},{4,8},{8,12},{12,16},{16,20},{20,24},{24,28},{28,32},{32,36}... | collective-permute-start | bytes 12296 | tf_op jit(solution)/shard_map/while/body/eval_jaxpr/ppermute | solution.py:17
  439.9 15.1 %collective-permute-start.9 = (f32[1024]{0:T(1024)S(1)}, f32[1024]{0:T(1024)S(1)}, u32[]{:S(2)}, u32[]{:S(2)}) collective-permute-start(f32[1024]{0:T(1024)S(1)} %get-tuple-element.2412), channel_id=1, source_target_pairs={{0,4},{4,8},{8,12},{12,16},{16,20},{20,24},{24,28},{28,32},{32,36}... | collective-permute-start | bytes 12296 | tf_op jit(solution)/shard_map/while/body/eval_jaxpr/ppermute | solution.py:17
  455.8 17.0 %collective-permute-start.7 = (bf16[1024,256]{1,0:T(8,128)(2,1)}, bf16[1024,256]{1,0:T(8,128)(2,1)S(1)}, u32[]{:S(2)}, u32[]{:S(2)}) collective-permute-start(bf16[1024,256]{1,0:T(8,128)(2,1)} %copy.96), channel_id=1, source_target_pairs={{0,4},{4,8},{8,12},{12,16},{16,20},{20,24},{24,28},{28,32},{32,36}... | collective-permute-start | bytes 1572872 | tf_op jit(solution)/shard_map/while/body/eval_jaxpr/ppermute | solution.py:17
  461.0 11.7 %collective-permute-start.8 = (f32[1024]{0:T(1024)S(1)}, f32[1024]{0:T(1024)S(1)}, u32[]{:S(2)}, u32[]{:S(2)}) collective-permute-start(f32[1024]{0:T(1024)S(1)} %get-tuple-element.2411), channel_id=1, source_target_pairs={{0,4},{4,8},{8,12},{12,16},{16,20},{20,24},{24,28},{28,32},{32,36}... | collective-permute-start | bytes 12296 | tf_op jit(solution)/shard_map/while/body/eval_jaxpr/ppermute | solution.py:17
  461.1 11.7 %collective-permute-start.9 = (f32[1024]{0:T(1024)S(1)}, f32[1024]{0:T(1024)S(1)}, u32[]{:S(2)}, u32[]{:S(2)}) collective-permute-start(f32[1024]{0:T(1024)S(1)} %get-tuple-element.2412), channel_id=1, source_target_pairs={{0,4},{4,8},{8,12},{12,16},{16,20},{20,24},{24,28},{28,32},{32,36}... | collective-permute-start | bytes 12296 | tf_op jit(solution)/shard_map/while/body/eval_jaxpr/ppermute | solution.py:17
  473.6 26.1 %collective-permute-start.7 = (bf16[1024,256]{1,0:T(8,128)(2,1)}, bf16[1024,256]{1,0:T(8,128)(2,1)S(1)}, u32[]{:S(2)}, u32[]{:S(2)}) collective-permute-start(bf16[1024,256]{1,0:T(8,128)(2,1)} %copy.96), channel_id=1, source_target_pairs={{0,4},{4,8},{8,12},{12,16},{16,20},{20,24},{24,28},{28,32},{32,36}... | collective-permute-start | bytes 1572872 | tf_op jit(solution)/shard_map/while/body/eval_jaxpr/ppermute | solution.py:17
  478.9 20.8 %collective-permute-start.8 = (f32[1024]{0:T(1024)S(1)}, f32[1024]{0:T(1024)S(1)}, u32[]{:S(2)}, u32[]{:S(2)}) collective-permute-start(f32[1024]{0:T(1024)S(1)} %get-tuple-element.2411), channel_id=1, source_target_pairs={{0,4},{4,8},{8,12},{12,16},{16,20},{20,24},{24,28},{28,32},{32,36}... | collective-permute-start | bytes 12296 | tf_op jit(solution)/shard_map/while/body/eval_jaxpr/ppermute | solution.py:17
  479.0 20.8 %collective-permute-start.9 = (f32[1024]{0:T(1024)S(1)}, f32[1024]{0:T(1024)S(1)}, u32[]{:S(2)}, u32[]{:S(2)}) collective-permute-start(f32[1024]{0:T(1024)S(1)} %get-tuple-element.2412), channel_id=1, source_target_pairs={{0,4},{4,8},{8,12},{12,16},{16,20},{20,24},{24,28},{28,32},{32,36}... | collective-permute-start | bytes 12296 | tf_op jit(solution)/shard_map/while/body/eval_jaxpr/ppermute | solution.py:17
  500.5 19.4 %collective-permute-start.7 = (bf16[1024,256]{1,0:T(8,128)(2,1)}, bf16[1024,256]{1,0:T(8,128)(2,1)S(1)}, u32[]{:S(2)}, u32[]{:S(2)}) collective-permute-start(bf16[1024,256]{1,0:T(8,128)(2,1)} %copy.96), channel_id=1, source_target_pairs={{0,4},{4,8},{8,12},{12,16},{16,20},{20,24},{24,28},{28,32},{32,36}... | collective-permute-start | bytes 1572872 | tf_op jit(solution)/shard_map/while/body/eval_jaxpr/ppermute | solution.py:17
  502.5 17.4 %collective-permute-start.8 = (f32[1024]{0:T(1024)S(1)}, f32[1024]{0:T(1024)S(1)}, u32[]{:S(2)}, u32[]{:S(2)}) collective-permute-start(f32[1024]{0:T(1024)S(1)} %get-tuple-element.2411), channel_id=1, source_target_pairs={{0,4},{4,8},{8,12},{12,16},{16,20},{20,24},{24,28},{28,32},{32,36}... | collective-permute-start | bytes 12296 | tf_op jit(solution)/shard_map/while/body/eval_jaxpr/ppermute | solution.py:17
  502.5 17.4 %collective-permute-start.9 = (f32[1024]{0:T(1024)S(1)}, f32[1024]{0:T(1024)S(1)}, u32[]{:S(2)}, u32[]{:S(2)}) collective-permute-start(f32[1024]{0:T(1024)S(1)} %get-tuple-element.2412), channel_id=1, source_target_pairs={{0,4},{4,8},{8,12},{12,16},{16,20},{20,24},{24,28},{28,32},{32,36}... | collective-permute-start | bytes 12296 | tf_op jit(solution)/shard_map/while/body/eval_jaxpr/ppermute | solution.py:17
  520.7 20.2 %collective-permute-start.7 = (bf16[1024,256]{1,0:T(8,128)(2,1)}, bf16[1024,256]{1,0:T(8,128)(2,1)S(1)}, u32[]{:S(2)}, u32[]{:S(2)}) collective-permute-start(bf16[1024,256]{1,0:T(8,128)(2,1)} %copy.96), channel_id=1, source_target_pairs={{0,4},{4,8},{8,12},{12,16},{16,20},{20,24},{24,28},{28,32},{32,36}... | collective-permute-start | bytes 1572872 | tf_op jit(solution)/shard_map/while/body/eval_jaxpr/ppermute | solution.py:17
  522.6 18.1 %collective-permute-start.8 = (f32[1024]{0:T(1024)S(1)}, f32[1024]{0:T(1024)S(1)}, u32[]{:S(2)}, u32[]{:S(2)}) collective-permute-start(f32[1024]{0:T(1024)S(1)} %get-tuple-element.2411), channel_id=1, source_target_pairs={{0,4},{4,8},{8,12},{12,16},{16,20},{20,24},{24,28},{28,32},{32,36}... | collective-permute-start | bytes 12296 | tf_op jit(solution)/shard_map/while/body/eval_jaxpr/ppermute | solution.py:17
  522.7 18.1 %collective-permute-start.9 = (f32[1024]{0:T(1024)S(1)}, f32[1024]{0:T(1024)S(1)}, u32[]{:S(2)}, u32[]{:S(2)}) collective-permute-start(f32[1024]{0:T(1024)S(1)} %get-tuple-element.2412), channel_id=1, source_target_pairs={{0,4},{4,8},{8,12},{12,16},{16,20},{20,24},{24,28},{28,32},{32,36}... | collective-permute-start | bytes 12296 | tf_op jit(solution)/shard_map/while/body/eval_jaxpr/ppermute | solution.py:17
  541.1 16.1 %collective-permute-start.17 = (f32[1024]{0:T(1024)S(1)}, f32[1024]{0:T(1024)S(1)}, u32[]{:S(2)}, u32[]{:S(2)}) collective-permute-start(f32[1024]{0:T(1024)S(1)} %get-tuple-element.1928), channel_id=1, source_target_pairs={{0,244},{4,248},{8,252},{12,0},{16,4},{20,8},{24,12},{28,16},{32,2... | collective-permute-start | bytes 12296 | tf_op jit(solution)/shard_map/ppermute | solution.py:17
  556.4 16.7 %collective-permute-start.18 = (f32[1024]{0:T(1024)S(1)}, f32[1024]{0:T(1024)S(1)}, u32[]{:S(2)}, u32[]{:S(2)}) collective-permute-start(f32[1024]{0:T(1024)S(1)} %get-tuple-element.1929), channel_id=1, source_target_pairs={{0,244},{4,248},{8,252},{12,0},{16,4},{20,8},{24,12},{28,16},{32,2... | collective-permute-start | bytes 12296 | tf_op jit(solution)/shard_map/ppermute | solution.py:17
  (14 other events, 113.3 us)
where the time goes:
time: 592 us; the launch traced here: 584 us
  waiting for transfers between devices  331 us (56%)
  starting transfers between devices  71.7 us (12%)
  blocking collectives  71.6 us (12%)
  other arithmetic  48.8 us (8%)
  local copies, waits for them, and re-layouts  29 us (5%)
  loops' own time  17.3 us (3%)
  matrix products  13.7 us (2%)
    ppermute x69, waiting for transfers between devices, shifted_2(): return lax.ppermute(value, axis, pairs)  331 us
    ppermute x69, starting transfers between devices, shifted_2(): return lax.ppermute(value, axis, pairs)  71.7 us
    all_gather x4, blocking collectives, merged(): gathered = jax.tree.map(lambda a: lax.all_gather(a, axis), part)  71.6 us
    reduce_or x25, other arithmetic, block_kept(): return jnp.any((row_ids == target_block) & in_use)  32.1 us
    another operation x42, local copies, waits for them, and re-layouts  26 us
    another operation x4, loops' own time, tour_targets(): lax.fori_loop(0, 2 * REACH, cycle_step, (running, message))  16.3 us
    dot_general x8, matrix products, scaled_cost(): lax.dot_general(src, tgt, (((1,), (1,)), ((), ())), preferred_element_typ...  13.7 us
  transfers between devices with their start and end apart: 69, of which 41 were waited for; matrix products, arithmetic and copies ran while one was open for 12% of the time, Pallas kernels for 0%

commit v1 on v0

v1 whole, which is shorter than its diff:
```python
import functools
import math

import jax
import jax.numpy as jnp
from jax import lax
from jax.experimental import pallas as pl
from jax.experimental.pallas import tpu as pltpu
from jax.sharding import PartitionSpec as P

ITERS = 2
EPS_START = 0.5
NEG_FILL = -1e30
LOG2E = math.log2(math.e)
LN2 = math.log(2.0)
REPS = 4
SEGMENT = 8
TAIL = 16


def send(value, place, blocks):
    pairs = []
    for block in range(blocks):
        for rep in range(REPS):
            to_block, to_rep = place(block, rep)
            pairs.append((block * REPS + rep, to_block % blocks * REPS + to_rep))
    return lax.ppermute(value, ("blk", "rep"), pairs)


def along(steps, blocks):
    def place(block, rep):
        target = (block + steps) % blocks
        return target, rep if (target // SEGMENT - block // SEGMENT) % 2 == 0 else REPS - 1 - rep

    return place


def by_core(even_steps, odd_steps, blocks):
    even, odd = along(even_steps, blocks), along(odd_steps, blocks)
    return lambda block, rep: even(block, rep) if block % 2 == 0 else odd(block, rep)


def sibling(block, rep):
    return block ^ 1, rep


def rep_xor(k):
    return lambda block, rep: (block, rep ^ k)


def half_norms(points):
    widened = points.astype(jnp.float32)
    return 0.5 * jnp.sum(widened * widened, axis=1)


def terms(vector):
    first = lax.reduce_precision(vector, 8, 7)
    rest = vector - first
    second = lax.reduce_precision(rest, 8, 7)
    third = lax.reduce_precision(rest - second, 8, 7)
    return [part.astype(jnp.bfloat16) for part in (first, second, third)]


def from_terms(rows):
    widened = rows.astype(jnp.float32)
    return widened[..., 0:2, :] + widened[..., 2:4, :] + widened[..., 4:6, :]


def log2_merge(*parts):
    top = functools.reduce(jnp.maximum, parts)
    return top + jnp.log2(sum(jnp.exp2(part - top) for part in parts))


def spread_rows(vector_ref, index, bias_ref):
    count = bias_ref.shape[0] // 128
    for q in range(count):
        row = vector_ref[index, q : q + 1, :]
        bias_ref[q * 128 : (q + 1) * 128, :] = jnp.broadcast_to(row, (128, 128)).T


def fold(value, combine):
    rows = value.shape[0]
    while rows > 8:
        rows //= 2
        value = combine(value[:rows], value[rows:])
    return value


def scores_into(score_ref, bias_ref, left_ref, left_at, left_rows, right_ref, right_rows, lane_at, scale):
    tops = []
    for c in range(0, right_rows, 256):
        right = right_ref[c : c + 256, :]
        top = None
        for r in range(0, left_rows, 256):
            cross = lax.dot_general(
                left_ref[r : r + 256, :], right, (((1,), (1,)), ((), ())), preferred_element_type=jnp.float32
            )
            bias = bias_ref[left_at + r : left_at + r + 256, :]
            scores = cross * scale + jnp.concatenate([bias, bias], axis=1)
            score_ref[left_at + r : left_at + r + 256, lane_at + c : lane_at + c + 256] = scores
            part = fold(scores, jnp.maximum)
            top = part if top is None else jnp.maximum(top, part)
        tops.append(top)
    return tops


def totals_of(score_ref, rows, lane_at, top):
    total = jnp.zeros_like(top)
    for r in range(0, rows, 64):
        scores = score_ref[r : r + 64, lane_at : lane_at + 256].reshape(8, 8, 256)
        total = total + jnp.sum(jnp.exp2(scores - top[None]), axis=0)
    return total


def row_kernel(scale, flags, own, mate, *refs):
    targets, (bias_in, out, bias, score, top_ref, total_ref) = refs[:7], refs[7:]
    top_ref[...] = jnp.full(top_ref.shape, NEG_FILL, jnp.float32)
    total_ref[...] = jnp.zeros(total_ref.shape, jnp.float32)
    half = own.shape[0]
    columns = bias.shape[0]
    for n in range(7):

        @pl.when(flags[n] != 0)
        def _(n=n):
            spread_rows(bias_in, n, bias)
            for side, src in enumerate((own, mate)):
                tops = scores_into(score, bias, targets[n], 0, columns, src, half, side * half, scale)
                for i, block_top in enumerate(tops):
                    at = side * half + i * 256
                    old = top_ref[:, at : at + 256]
                    top = jnp.maximum(old, block_top)
                    total = totals_of(score, columns, at, top)
                    total_ref[:, at : at + 256] = total_ref[:, at : at + 256] * jnp.exp2(old - top) + total
                    top_ref[:, at : at + 256] = top

    top = top_ref[...]
    greatest = jnp.max(top, axis=0, keepdims=True)
    total = jnp.sum(total_ref[...] * jnp.exp2(top - greatest), axis=0, keepdims=True)
    out[...] = greatest + jnp.log2(total)


def column_kernel(scale, flags, own, mate, *refs):
    targets, (bias_in, out, bias, score) = refs[:7], refs[7:]
    out[...] = jnp.full(out.shape, NEG_FILL, jnp.float32)
    spread_rows(bias_in, 0, bias)
    half = own.shape[0]
    for n in range(7):

        @pl.when(flags[n] != 0)
        def _(n=n):
            columns = out.shape[1]
            first = scores_into(score, bias, own, 0, half, targets[n], columns, 0, scale)
            second = scores_into(score, bias, mate, half, half, targets[n], columns, 0, scale)
            for i, (a, b) in enumerate(zip(first, second)):
                top = jnp.max(jnp.maximum(a, b), axis=0, keepdims=True)
                total = totals_of(score, 2 * half, i * 256, jnp.broadcast_to(top, (8, 256)))
                total = jnp.sum(total, axis=0, keepdims=True)
                out[pl.ds(flags[7 + n], 1), i * 256 : (i + 1) * 256] = top + jnp.log2(total)


def call_rows(scale, flags, own, mate, targets, bias):
    half, columns = own.shape[0], targets[0].shape[0] - TAIL
    whole = pl.BlockSpec(memory_space=pltpu.VMEM)
    return pl.pallas_call(
        functools.partial(row_kernel, scale),
        out_shape=jax.ShapeDtypeStruct((1, 2 * half), jnp.float32),
        in_specs=[pl.BlockSpec(memory_space=pltpu.SMEM)] + [whole] * 10,
        out_specs=whole,
        scratch_shapes=[
            pltpu.VMEM((columns, 128), jnp.float32),
            pltpu.VMEM((columns, 2 * half), jnp.float32),
            pltpu.VMEM((8, 2 * half), jnp.float32),
            pltpu.VMEM((8, 2 * half), jnp.float32),
        ],
        compiler_params=pltpu.CompilerParams(vmem_limit_bytes=32 * 2**20),
        name="rows",
    )(flags, own, mate, *targets, bias)


def call_columns(scale, flags, own, mate, targets, bias):
    half, columns = own.shape[0], targets[0].shape[0] - TAIL
    whole = pl.BlockSpec(memory_space=pltpu.VMEM)
    return pl.pallas_call(
        functools.partial(column_kernel, scale),
        out_shape=jax.ShapeDtypeStruct((8, columns), jnp.float32),
        in_specs=[pl.BlockSpec(memory_space=pltpu.SMEM)] + [whole] * 10,
        out_specs=whole,
        scratch_shapes=[
            pltpu.VMEM((2 * half, 128), jnp.float32),
            pltpu.VMEM((2 * half, columns), jnp.float32),
        ],
        compiler_params=pltpu.CompilerParams(vmem_limit_bytes=32 * 2**20),
        name="columns",
    )(flags, own, mate, *targets, bias)


def fill_rows(value, before, after):
    return jnp.pad(value, ((before, after), (0, 0)), constant_values=NEG_FILL)


def local(src_points, src_log_mass, tgt_points, tgt_log_mass, initial_potential, pair_list, pair_count):
    block = lax.axis_index("blk")
    rep = lax.axis_index("rep")
    blocks = lax.axis_size("blk")
    core = block % 2
    half_index = (rep % 2) ^ ((block // SEGMENT) % 2)
    rows = src_points.shape[0]
    width = tgt_points.shape[0]
    columns = width // 2

    def my_half(value):
        return lax.dynamic_slice_in_dim(value, half_index * columns, columns, 0)

    first_scale = LOG2E / EPS_START
    points = my_half(tgt_points)
    masses = my_half(tgt_log_mass) * LOG2E
    bias = masses + (my_half(initial_potential) - half_norms(points)) * first_scale
    tail = [part.reshape(-1, points.shape[1]) for part in terms(bias) + terms(masses)]
    tail.append(jnp.zeros((TAIL - 6 * columns // points.shape[1], points.shape[1]), jnp.bfloat16))
    message = jnp.concatenate([points] + tail, axis=0)

    before = send(message, along(2, blocks), blocks)
    after = send(message, along(-2, blocks), blocks)
    third = send(message, by_core(-3, 3, blocks), blocks)
    beside = send(message, sibling, blocks)
    mate = send(src_points, rep_xor(1), blocks)
    before_beside = send(before, sibling, blocks)
    after_beside = send(after, sibling, blocks)
    targets = [message, beside, before, before_beside, after, after_beside, third]

    even_slots = jnp.array([3, 4, 1, 2, 5, 6, 0], jnp.int32)
    odd_slots = jnp.array([4, 3, 2, 1, 6, 5, 7], jnp.int32)
    slots = jnp.where(core == 0, even_slots, odd_slots)
    names = (block - core - 3 + slots) % blocks
    row_names = pair_list[block]
    in_use = jnp.arange(row_names.shape[0], dtype=jnp.int32) < pair_count[block]
    kept = jnp.any((row_names[None, :] == names[:, None]) & in_use[None, :], axis=1)
    flags = jnp.concatenate([kept.astype(jnp.int32), slots])

    tails = jnp.stack([target[columns:] for target in targets])
    biases = from_terms(tails[:, 0:6]).reshape(7, columns // 128, 128)
    window_masses = from_terms(tails[:, 6:12]).reshape(7, columns // 128, 128)
    src_masses = src_log_mass * LOG2E

    for sweep in range(ITERS):
        epsilon = EPS_START * 0.5**sweep
        scale = LOG2E / epsilon
        part = call_rows(scale, flags, src_points, mate, targets, biases).reshape(-1)
        if sweep == 0:
            got = send(jnp.concatenate([part, src_masses]), rep_xor(1), blocks)
            both_masses = jnp.concatenate([src_masses, got[2 * rows :]])
        else:
            got = send(part, rep_xor(1), blocks)
        row_sums = log2_merge(part, jnp.concatenate([got[rows : 2 * rows], got[:rows]]))
        weighted = (both_masses - row_sums).reshape(1, 2 * rows // 128, 128)
        part = call_columns(scale, flags, src_points, mate, targets, weighted)
        chip = log2_merge(
            part,
            send(part, sibling, blocks),
            send(part, rep_xor(2), blocks),
            send(part, lambda b, r: (b ^ 1, r ^ 2), blocks),
        )
        forward = core == 0
        if sweep + 1 < ITERS:
            got = []
            for n in (1, 2, 3):
                kept_rows = 8 - 2 * n
                out = jnp.where(forward, chip[2 * n :], chip[:kept_rows])
                out = send(out, by_core(2 * n, -2 * n, blocks), blocks)
                got.append(
                    jnp.where(forward, fill_rows(out, 0, 2 * n), fill_rows(out, 2 * n, 0))
                )
            side = log2_merge(*got)
            column_sums = log2_merge(chip, side, send(side, sibling, blocks))
            mine = jnp.where(
                core == 0,
                jnp.stack([column_sums[i] for i in (3, 4, 1, 2, 5, 6, 0)]),
                jnp.stack([column_sums[i] for i in (4, 3, 2, 1, 6, 5, 7)]),
            )
            biases = window_masses - 2.0 * mine.reshape(7, columns // 128, 128)
        else:
            near = jnp.where(forward, chip[5:7], chip[1:3])
            near = send(near, by_core(2, -2, blocks), blocks)
            far = jnp.where(forward, chip[7], chip[0])
            far = send(far, by_core(4, -4, blocks), blocks)
            empty = jnp.full_like(far, NEG_FILL)
            far = jnp.where(forward, jnp.stack([far, empty]), jnp.stack([empty, far]))
            side = log2_merge(near, far)
            column_sums = log2_merge(chip[3:5], side, send(side, sibling, blocks))
            mine = jnp.where(core == 0, column_sums[0], column_sums[1])
            other = send(mine, rep_xor(1), blocks)
            whole = jnp.where(
                half_index == 0, jnp.concatenate([mine, other]), jnp.concatenate([other, mine])
            )
            source_pot = half_norms(src_points) - (epsilon * LN2) * row_sums[:rows]
            target_pot = half_norms(tgt_points) - (epsilon * LN2) * whole
    return source_pot, target_pot


def solution(mesh):
    in_specs = (
        P(("blk", "rep"), None),
        P(("blk", "rep")),
        P("blk", None),
        P("blk"),
        P("blk"),
        P(),
        P(),
    )
    out_specs = (P(("blk", "rep")), P("blk"))
    return jax.shard_map(local, mesh=mesh, in_specs=in_specs, out_specs=out_specs, check_vma=False)
```

time: 592 us -> 94.6 us (0.16); the launches traced: 584 us -> 93.7 us
  waiting for transfers between devices: 331 us -> 26.3 us
  blocking collectives: 71.6 us -> 0 us
  other arithmetic: 48.8 us -> 4.05 us
  local copies, waits for them, and re-layouts: 29 us -> 3.07 us
  starting transfers between devices: 71.7 us -> 46.4 us
  loops' own time: 17.3 us -> 0 us
  matrix products: 13.7 us -> 0 us
  Pallas kernels: 0 us -> 12.8 us
    ppermute x69 -> x23, waiting for transfers between devices: 331 us -> 26.3 us  [send(): return lax.ppermute(value, ('blk', 'rep'), pairs)]
    all_gather x4 -> x0, blocking collectives: 71.6 us -> none  [merged(): gathered = jax.tree.map(lambda a: lax.all_gather(a, axis), part)]
    reduce_or x25 -> x1, other arithmetic: 32.1 us -> 0.19 us  [local(): jnp.any((row_names[None, :] == names[:, None]) & in_use[None, :], axis=1)]
    another operation x42 -> x5, local copies, waits for them, and re-layouts: 26 us -> 0.05 us  [the longest x3 0.04 us: local(): jnp.stack([column_sums[i] for i in (3, 4, 1, 2, 5, 6, 0)])]
    ppermute x69 -> x23, starting transfers between devices: 71.7 us -> 46.4 us  [send(): return lax.ppermute(value, ('blk', 'rep'), pairs)]
    another operation x34 -> x0, loops' own time: 17.3 us -> none  [the longest x4 16.3 us: tour_targets(): lax.fori_loop(0, 2 * REACH, cycle_step, (running, message))]
    dot_general x8 -> x0, matrix products: 13.7 us -> none  [scaled_cost(): lax.dot_general(src, tgt, (((1,), (1,)), ((), ())), preferred_element_typ...]
    pallas_call x0 -> x4, Pallas kernels: none -> 12.8 us  [the longest x2 6.66 us: call_columns(): pl.pallas_call(functools.partial(column_kernel, scale), out_shape=jax.Sha...]
  transfers between devices with their start and end apart: 69 -> 23, of which waited for: 41 -> 15; matrix products, arithmetic and copies ran while one was open for 12% -> 3% of each run, Pallas kernels for 0% -> 0%
where the time goes in v1:
time: 94.6 us; the launch traced here: 93.7 us
  starting transfers between devices  46.4 us (49%)
  waiting for transfers between devices  26.3 us (28%)
  Pallas kernels  12.8 us (14%)
  other arithmetic  4.05 us (4%)
  local copies, waits for them, and re-layouts  3.07 us (3%)
  between operations  1.03 us (1%)
    ppermute x23, starting transfers between devices, send(): return lax.ppermute(value, ('blk', 'rep'), pairs)  46.4 us
    ppermute x23, waiting for transfers between devices, send(): return lax.ppermute(value, ('blk', 'rep'), pairs)  26.3 us
    pallas_call x2, Pallas kernels, call_columns(): pl.pallas_call(functools.partial(column_kernel, scale), out_shape=jax.Sha...  6.66 us
    pallas_call x2, Pallas kernels, call_rows(): pl.pallas_call(functools.partial(row_kernel, scale), out_shape=jax.ShapeD...  6.18 us
  transfers between devices with their start and end apart: 23, of which 15 were waited for; matrix products, arithmetic and copies ran while one was open for 3% of the time, Pallas kernels for 0%

profile of v1, /device:TPU:1, one launch (start us, length us, event | category | flops | bytes accessed | tf_op | source)
XLA Modules:
  0.0 93.7 jit_solution(642451096205492992)
XLA Ops:
  0.6 0.0 copy-start
  0.7 1.1 %multiply_reduce_fusion.1 = (f32[512]{0:T(512)S(1)}, bf16[512,256]{1,0:T(8,128)(2,1)S(1)}) fusion(bf16[1024,256]{1,0:T(8,128)(2,1)} %param.11, s32[]{:T(128)S(6)} %select_n.133), kind=kLoop, calls=%fused_computation.1 | loop fusion | flops 392704 | bytes 526340 | tf_op jit(solution)/shard_map/reduce_sum | solution.py:53
  1.8 0.1 fusion.15
  2.0 0.1 concatenate.80.refs_0_
  2.2 3.3 %collective-permute-start.1 = (bf16[528,256]{1,0:T(8,128)(2,1)S(1)}, bf16[528,256]{1,0:T(8,128)(2,1)S(1)}, u32[]{:S(2)}, u32[]{:S(2)}) collective-permute-start(bf16[528,256]{1,0:T(8,128)(2,1)S(1)} %concatenate.80.refs_0_), channel_id=1, source_target_pairs={{0,4},{1,5},{2,6},{3,7},{4,0},{5,1},{6,2},{7,3},{8,12},{9,13},{10,... | collective-permute-start | bytes 811016 | tf_op jit(solution)/shard_map/ppermute | solution.py:27
  5.5 0.0 collective-permute-start.2
  5.5 8.5 %collective-permute-start.4 = (bf16[528,256]{1,0:T(8,128)(2,1)S(1)}, bf16[528,256]{1,0:T(8,128)(2,1)S(1)}, u32[]{:S(2)}, u32[]{:S(2)}) collective-permute-start(bf16[528,256]{1,0:T(8,128)(2,1)S(1)} %concatenate.80.refs_0_), channel_id=1, source_target_pairs={{0,251},{1,250},{2,249},{3,248},{4,255},{5,254},{6,253},{7,252},{8... | collective-permute-start | bytes 811016 | tf_op jit(solution)/shard_map/ppermute | solution.py:27
  14.0 1.6 %collective-permute-start = (bf16[512,256]{1,0:T(8,128)(2,1)S(1)}, bf16[512,256]{1,0:T(8,128)(2,1)S(1)}, u32[]{:S(2)}, u32[]{:S(2)}) collective-permute-start(bf16[512,256]{1,0:T(8,128)(2,1)S(1)} %copy-done.1), channel_id=1, source_target_pairs={{0,1},{1,0},{2,3},{3,2},{4,5},{5,4},{6,7},{7,6},{8,9},{9,8},{10,11... | collective-permute-start | bytes 786440 | tf_op jit(solution)/shard_map/ppermute | solution.py:27
  15.6 0.7 copy-done.8
  16.3 0.6 dynamic_slice.16
  16.9 0.6 iota_compare_fusion
  17.5 0.2 dynamic-slice_reduce_fusion
  17.7 0.0 copy-start.7
  17.7 0.6 copy-done.6
  18.4 0.0 copy-done.7
  18.4 0.0 copy-start.3
  18.4 0.2 and_reduce_fusion
  18.6 0.5 copy-done.3
  19.1 0.1 pad_add_fusion.flags
  19.2 10.7 %collective-permute-done.2.refs_2_ = bf16[528,256]{1,0:T(8,128)(2,1)S(1)} collective-permute-done((bf16[528,256]{1,0:T(8,128)(2,1)S(1)}, bf16[528,256]{1,0:T(8,128)(2,1)S(1)}, u32[]{:S(2)}, u32[]{:S(2)}) %collective-permute-start.2) | collective-permute-done | bytes 270368 | tf_op jit(solution)/shard_map/ppermute | solution.py:27
  29.9 1.2 %collective-permute-start.3 = (bf16[528,256]{1,0:T(8,128)(2,1)S(1)}, bf16[528,256]{1,0:T(8,128)(2,1)S(1)}, u32[]{:S(2)}, u32[]{:S(2)}) collective-permute-start(bf16[528,256]{1,0:T(8,128)(2,1)S(1)} %collective-permute-done.2.refs_2_), channel_id=1, source_target_pairs={{0,4},{1,5},{2,6},{3,7},{4,0},{5,1},{6,2},{7,3},{8,12},{9,13},{10,... | collective-permute-start | bytes 811016 | tf_op jit(solution)/shard_map/ppermute | solution.py:27
  31.1 0.0 collective-permute-done.4.refs_4_
  31.1 0.0 collective-permute-start.5
  31.1 1.1 %collective-permute-done.3.refs_3_ = bf16[528,256]{1,0:T(8,128)(2,1)S(1)} collective-permute-done((bf16[528,256]{1,0:T(8,128)(2,1)S(1)}, bf16[528,256]{1,0:T(8,128)(2,1)S(1)}, u32[]{:S(2)}, u32[]{:S(2)}) %collective-permute-start.3) | collective-permute-done | bytes 270368 | tf_op jit(solution)/shard_map/ppermute | solution.py:27
  32.2 0.4 collective-permute-done.5.refs_5_
  32.6 0.0 collective-permute-done.6.refs_6_
  32.7 3.0 %rows.2 = f32[1,1024]{1,0:T(1,128)S(1)} custom-call(s32[14]{0:T(128)S(1)} %pad_add_fusion.flags, bf16[512,256]{1,0:T(8,128)(2,1)S(1)} %copy-done.1, bf16[512,256]{1,0:T(8,128)(2,1)S(1)} %collective-permute-done.mate, bf16[528,256]{1,0:T(8,128)(2,1)S(1)} %concatenate.80.refs_0_, bf16[528,256]{1,0:T(8,128)(2,1)S(1)} %collective-permute-done.1.refs_1_, ...), custom_call_target="tpu_custom_call" | custom-call | tf_op jit(solution)/shard_map/rows/pallas_call | solution.py:164
  35.7 0.1 collective-permute-start.7
  35.8 2.5 %collective-permute-done.7 = f32[1536]{0:T(1024)S(1)} collective-permute-done((f32[1536]{0:T(1024)S(1)}, f32[1536]{0:T(1024)S(1)}, u32[]{:S(2)}, u32[]{:S(2)}) %collective-permute-start.7) | collective-permute-done | bytes 6176 | tf_op jit(solution)/shard_map/ppermute | solution.py:27
  38.3 3.4 %columns.2 = f32[8,512]{1,0:T(8,128)S(1)} custom-call(s32[14]{0:T(128)S(1)} %pad_add_fusion.flags, bf16[512,256]{1,0:T(8,128)(2,1)S(1)} %copy-done.1, bf16[512,256]{1,0:T(8,128)(2,1)S(1)} %collective-permute-done.mate, bf16[528,256]{1,0:T(8,128)(2,1)S(1)} %concatenate.80.refs_0_, bf16[528,256]{1,0:T(8,128)(2,1)S(1)} %collective-permute-done.1.refs_1_, ...), custom_call_target="tpu_custom_call" | custom-call | tf_op jit(solution)/shard_map/columns/pallas_call | solution.py:183
  41.7 0.1 collective-permute-start.10
  41.8 0.8 collective-permute-start.8
  42.7 1.9 %collective-permute-start.9 = (f32[8,512]{1,0:T(8,128)S(1)}, f32[8,512]{1,0:T(8,128)S(1)}, u32[]{:S(2)}, u32[]{:S(2)}) collective-permute-start(f32[8,512]{1,0:T(8,128)S(1)} %columns.2), channel_id=1, source_target_pairs={{0,2},{1,3},{2,0},{3,1},{4,6},{5,7},{6,4},{7,5},{8,10},{9,11},{10,... | collective-permute-start | bytes 49160 | tf_op jit(solution)/shard_map/ppermute | solution.py:27
  44.6 1.3 %collective-permute-done.10 = f32[8,512]{1,0:T(8,128)S(1)} collective-permute-done((f32[8,512]{1,0:T(8,128)S(1)}, f32[8,512]{1,0:T(8,128)S(1)}, u32[]{:S(2)}, u32[]{:S(2)}) %collective-permute-start.10) | collective-permute-done | bytes 16416 | tf_op jit(solution)/shard_map/ppermute | solution.py:27
  45.9 0.0 collective-permute-done.8
  45.9 0.3 collective-permute-done.9
  46.2 6.5 %collective-permute-start.11 = (f32[6,512]{1,0:T(8,128)S(1)}, f32[6,512]{1,0:T(8,128)S(1)}, u32[]{:S(2)}, u32[]{:S(2)}) collective-permute-start(f32[6,512]{1,0:T(8,128)S(1)} %slice_select_fusion), channel_id=1, source_target_pairs={{0,8},{1,9},{2,10},{3,11},{4,255},{5,254},{6,253},{7,252},{8,16},{... | collective-permute-start | bytes 36872 | tf_op jit(solution)/shard_map/ppermute | solution.py:27
  52.7 0.0 collective-permute-start.12
  52.7 1.2 %collective-permute-start.13 = (f32[2,512]{1,0:T(2,128)S(1)}, f32[2,512]{1,0:T(2,128)S(1)}, u32[]{:S(2)}, u32[]{:S(2)}) collective-permute-start(f32[2,512]{1,0:T(2,128)S(1)} %slice_select_fusion.3), channel_id=1, source_target_pairs={{0,24},{1,25},{2,26},{3,27},{4,239},{5,238},{6,237},{7,236},{8,35}... | collective-permute-start | bytes 12296 | tf_op jit(solution)/shard_map/ppermute | solution.py:27
  54.0 2.8 %collective-permute-done.13 = f32[2,512]{1,0:T(2,128)S(1)} collective-permute-done((f32[2,512]{1,0:T(2,128)S(1)}, f32[2,512]{1,0:T(2,128)S(1)}, u32[]{:S(2)}, u32[]{:S(2)}) %collective-permute-start.13) | collective-permute-done | bytes 4128 | tf_op jit(solution)/shard_map/ppermute | solution.py:27
  56.8 0.2 collective-permute-done.12
  57.1 1.4 %collective-permute-start.14 = (f32[8,512]{1,0:T(8,128)S(1)}, f32[8,512]{1,0:T(8,128)S(1)}, u32[]{:S(2)}, u32[]{:S(2)}) collective-permute-start(f32[8,512]{1,0:T(8,128)S(1)} %multiply_add_fusion.2), channel_id=1, source_target_pairs={{0,4},{1,5},{2,6},{3,7},{4,0},{5,1},{6,2},{7,3},{8,12},{9,13},{10,... | collective-permute-start | bytes 49160 | tf_op jit(solution)/shard_map/ppermute | solution.py:27
  58.6 0.8 collective-permute-done.14
  59.6 3.2 %rows.3 = f32[1,1024]{1,0:T(1,128)S(1)} custom-call(s32[14]{0:T(128)S(1)} %pad_add_fusion.flags, bf16[512,256]{1,0:T(8,128)(2,1)S(1)} %copy-done.1, bf16[512,256]{1,0:T(8,128)(2,1)S(1)} %collective-permute-done.mate, bf16[528,256]{1,0:T(8,128)(2,1)S(1)} %concatenate.80.refs_0_, bf16[528,256]{1,0:T(8,128)(2,1)S(1)} %collective-permute-done.1.refs_1_, ...), custom_call_target="tpu_custom_call" | custom-call | tf_op jit(solution)/shard_map/rows/pallas_call | solution.py:164
  62.8 3.6 %collective-permute-start.15 = (f32[1024]{0:T(1024)S(1)}, f32[1024]{0:T(1024)S(1)}, u32[]{:S(2)}, u32[]{:S(2)}) collective-permute-start(f32[1024]{0:T(1024)S(1)} %bitcast.54), channel_id=1, source_target_pairs={{0,1},{1,0},{2,3},{3,2},{4,5},{5,4},{6,7},{7,6},{8,9},{9,8},{10,11... | collective-permute-start | bytes 12296 | tf_op jit(solution)/shard_map/ppermute | solution.py:27
  66.4 1.0 %collective-permute-done.15 = f32[1024]{0:T(1024)S(1)} collective-permute-done((f32[1024]{0:T(1024)S(1)}, f32[1024]{0:T(1024)S(1)}, u32[]{:S(2)}, u32[]{:S(2)}) %collective-permute-start.15) | collective-permute-done | bytes 4128 | tf_op jit(solution)/shard_map/ppermute | solution.py:27
  67.4 3.2 %columns.3 = f32[8,512]{1,0:T(8,128)S(1)} custom-call(s32[14]{0:T(128)S(1)} %pad_add_fusion.flags, bf16[512,256]{1,0:T(8,128)(2,1)S(1)} %copy-done.1, bf16[512,256]{1,0:T(8,128)(2,1)S(1)} %collective-permute-done.mate, bf16[528,256]{1,0:T(8,128)(2,1)S(1)} %concatenate.80.refs_0_, bf16[528,256]{1,0:T(8,128)(2,1)S(1)} %collective-permute-done.1.refs_1_, ...), custom_call_target="tpu_custom_call" | custom-call | tf_op jit(solution)/shard_map/columns/pallas_call | solution.py:183
  70.6 0.1 collective-permute-start.16
  70.7 2.0 %collective-permute-start.17 = (f32[8,512]{1,0:T(8,128)S(1)}, f32[8,512]{1,0:T(8,128)S(1)}, u32[]{:S(2)}, u32[]{:S(2)}) collective-permute-start(f32[8,512]{1,0:T(8,128)S(1)} %columns.3), channel_id=1, source_target_pairs={{0,2},{1,3},{2,0},{3,1},{4,6},{5,7},{6,4},{7,5},{8,10},{9,11},{10,... | collective-permute-start | bytes 49160 | tf_op jit(solution)/shard_map/ppermute | solution.py:27
  72.7 1.0 %collective-permute-start.18 = (f32[8,512]{1,0:T(8,128)S(1)}, f32[8,512]{1,0:T(8,128)S(1)}, u32[]{:S(2)}, u32[]{:S(2)}) collective-permute-start(f32[8,512]{1,0:T(8,128)S(1)} %columns.3), channel_id=1, source_target_pairs={{0,6},{1,7},{2,4},{3,5},{4,2},{5,3},{6,0},{7,1},{8,14},{9,15},{10,... | collective-permute-start | bytes 49160 | tf_op jit(solution)/shard_map/ppermute | solution.py:27
  73.8 0.2 multiply_reduce_fusion
  74.0 0.3 collective-permute-done.17
  74.3 3.0 %collective-permute-done.18 = f32[8,512]{1,0:T(8,128)S(1)} collective-permute-done((f32[8,512]{1,0:T(8,128)S(1)}, f32[8,512]{1,0:T(8,128)S(1)}, u32[]{:S(2)}, u32[]{:S(2)}) %collective-permute-start.18) | collective-permute-done | bytes 16416 | tf_op jit(solution)/shard_map/ppermute | solution.py:27
  77.4 4.3 %collective-permute-start.20 = (f32[512]{0:T(512)S(1)}, f32[512]{0:T(512)S(1)}, u32[]{:S(2)}, u32[]{:S(2)}) collective-permute-start(f32[512]{0:T(512)S(1)} %bitcast.71), channel_id=1, source_target_pairs={{0,16},{1,17},{2,18},{3,19},{4,247},{5,246},{6,245},{7,244},{8,24}... | collective-permute-start | bytes 6152 | tf_op jit(solution)/shard_map/ppermute | solution.py:27
  81.7 1.9 %collective-permute-start.19 = (f32[2,512]{1,0:T(2,128)S(1)}, f32[2,512]{1,0:T(2,128)S(1)}, u32[]{:S(2)}, u32[]{:S(2)}) collective-permute-start(f32[2,512]{1,0:T(2,128)S(1)} %slice_select_fusion.2), channel_id=1, source_target_pairs={{0,8},{1,9},{2,10},{3,11},{4,255},{5,254},{6,253},{7,252},{8,16},{... | collective-permute-start | bytes 12296 | tf_op jit(solution)/shard_map/ppermute | solution.py:27
  83.6 0.1 multiply_reduce_fusion.2
  83.8 0.7 collective-permute-done.19
  84.5 5.0 %collective-permute-start.21 = (f32[2,512]{1,0:T(2,128)S(1)}, f32[2,512]{1,0:T(2,128)S(1)}, u32[]{:S(2)}, u32[]{:S(2)}) collective-permute-start(f32[2,512]{1,0:T(2,128)S(1)} %multiply_add_fusion.5), channel_id=1, source_target_pairs={{0,4},{1,5},{2,6},{3,7},{4,0},{5,1},{6,2},{7,3},{8,12},{9,13},{10,... | collective-permute-start | bytes 12296 | tf_op jit(solution)/shard_map/ppermute | solution.py:27
  89.5 0.8 collective-permute-done.21
  90.3 0.1 multiply_add_fusion.4
  90.3 1.8 %collective-permute-start.22 = (f32[512]{0:T(512)S(1)}, f32[512]{0:T(512)S(1)}, u32[]{:S(2)}, u32[]{:S(2)}) collective-permute-start(f32[512]{0:T(512)S(1)} %bitcast.66), channel_id=1, source_target_pairs={{0,1},{1,0},{2,3},{3,2},{4,5},{5,4},{6,7},{7,6},{8,9},{9,8},{10,11... | collective-permute-start | bytes 6152 | tf_op jit(solution)/shard_map/ppermute | solution.py:27
  92.1 0.6 multiply_subtract_fusion
  92.7 0.4 collective-permute-done.22
  93.1 0.6 fusion.3
  (71 shorter events, 0.7 us)
Async XLA Ops:
  0.6 16.9 %copy-start = (s32[64,7]{0,1:T(8,128)S(1)}, s32[64,7]{0,1:T(8,128)}, u32[]{:S(2)}) copy-start(s32[64,7]{0,1:T(8,128)} %param.14) | copy-start | bytes 5380
  0.7 1.1 %copy-start.4 = (f32[1024]{0:T(1024)S(1)}, f32[1024]{0:T(1024)}, u32[]{:S(2)}) copy-start(f32[1024]{0:T(1024)} %param.12) | copy-start | bytes 12292
  0.7 1.1 %copy-start.5 = (f32[1024]{0:T(1024)S(1)}, f32[1024]{0:T(1024)}, u32[]{:S(2)}) copy-start(f32[1024]{0:T(1024)} %param.13) | copy-start | bytes 12292
  2.0 12.0 %copy-start.1 = (bf16[512,256]{1,0:T(8,128)(2,1)S(1)}, bf16[512,256]{1,0:T(8,128)(2,1)}, u32[]{:S(2)}) copy-start(bf16[512,256]{1,0:T(8,128)(2,1)} %own.7) | copy-start | bytes 786436
  2.2 28.9 %collective-permute-start.1 = (bf16[528,256]{1,0:T(8,128)(2,1)S(1)}, bf16[528,256]{1,0:T(8,128)(2,1)S(1)}, u32[]{:S(2)}, u32[]{:S(2)}) collective-permute-start(bf16[528,256]{1,0:T(8,128)(2,1)S(1)} %concatenate.80.refs_0_), channel_id=1, source_target_pairs={{0,4},{1,5},{2,6},{3,7},{4,0},{5,1},{6,2},{7,3},{8,12},{9,13},{10,... | collective-permute-start | bytes 811016 | tf_op jit(solution)/shard_map/ppermute | solution.py:27
  5.5 24.4 %collective-permute-start.2 = (bf16[528,256]{1,0:T(8,128)(2,1)S(1)}, bf16[528,256]{1,0:T(8,128)(2,1)S(1)}, u32[]{:S(2)}, u32[]{:S(2)}) collective-permute-start(bf16[528,256]{1,0:T(8,128)(2,1)S(1)} %concatenate.80.refs_0_), channel_id=1, source_target_pairs={{0,8},{1,9},{2,10},{3,11},{4,12},{5,13},{6,14},{7,15},{8,16},{9,17... | collective-permute-start | bytes 811016 | tf_op jit(solution)/shard_map/ppermute | solution.py:27
  5.5 25.6 %collective-permute-start.4 = (bf16[528,256]{1,0:T(8,128)(2,1)S(1)}, bf16[528,256]{1,0:T(8,128)(2,1)S(1)}, u32[]{:S(2)}, u32[]{:S(2)}) collective-permute-start(bf16[528,256]{1,0:T(8,128)(2,1)S(1)} %concatenate.80.refs_0_), channel_id=1, source_target_pairs={{0,251},{1,250},{2,249},{3,248},{4,255},{5,254},{6,253},{7,252},{8... | collective-permute-start | bytes 811016 | tf_op jit(solution)/shard_map/ppermute | solution.py:27
  14.0 18.6 %collective-permute-start.6 = (bf16[528,256]{1,0:T(8,128)(2,1)S(1)}, bf16[528,256]{1,0:T(8,128)(2,1)S(1)}, u32[]{:S(2)}, u32[]{:S(2)}) collective-permute-start(bf16[528,256]{1,0:T(8,128)(2,1)S(1)} %concatenate.80.refs_0_), channel_id=1, source_target_pairs={{0,247},{1,246},{2,245},{3,244},{4,16},{5,17},{6,18},{7,19},{8,255... | collective-permute-start | bytes 811016 | tf_op jit(solution)/shard_map/ppermute | solution.py:27
  14.0 18.7 %collective-permute-start = (bf16[512,256]{1,0:T(8,128)(2,1)S(1)}, bf16[512,256]{1,0:T(8,128)(2,1)S(1)}, u32[]{:S(2)}, u32[]{:S(2)}) collective-permute-start(bf16[512,256]{1,0:T(8,128)(2,1)S(1)} %copy-done.1), channel_id=1, source_target_pairs={{0,1},{1,0},{2,3},{3,2},{4,5},{5,4},{6,7},{7,6},{8,9},{9,8},{10,11... | collective-permute-start | bytes 786440 | tf_op jit(solution)/shard_map/ppermute | solution.py:27
  15.6 0.7 copy-start.8
  17.7 0.7 copy-start.6
  17.7 0.7 copy-start.7
  18.4 0.7 copy-start.3
  29.9 2.3 %collective-permute-start.3 = (bf16[528,256]{1,0:T(8,128)(2,1)S(1)}, bf16[528,256]{1,0:T(8,128)(2,1)S(1)}, u32[]{:S(2)}, u32[]{:S(2)}) collective-permute-start(bf16[528,256]{1,0:T(8,128)(2,1)S(1)} %collective-permute-done.2.refs_2_), channel_id=1, source_target_pairs={{0,4},{1,5},{2,6},{3,7},{4,0},{5,1},{6,2},{7,3},{8,12},{9,13},{10,... | collective-permute-start | bytes 811016 | tf_op jit(solution)/shard_map/ppermute | solution.py:27
  31.1 1.6 %collective-permute-start.5 = (bf16[528,256]{1,0:T(8,128)(2,1)S(1)}, bf16[528,256]{1,0:T(8,128)(2,1)S(1)}, u32[]{:S(2)}, u32[]{:S(2)}) collective-permute-start(bf16[528,256]{1,0:T(8,128)(2,1)S(1)} %collective-permute-done.4.refs_4_), channel_id=1, source_target_pairs={{0,4},{1,5},{2,6},{3,7},{4,0},{5,1},{6,2},{7,3},{8,12},{9,13},{10,... | collective-permute-start | bytes 811016 | tf_op jit(solution)/shard_map/ppermute | solution.py:27
  35.7 2.6 %collective-permute-start.7 = (f32[1536]{0:T(1024)S(1)}, f32[1536]{0:T(1024)S(1)}, u32[]{:S(2)}, u32[]{:S(2)}) collective-permute-start(f32[1536]{0:T(1024)S(1)} %pad_maximum_fusion), channel_id=1, source_target_pairs={{0,1},{1,0},{2,3},{3,2},{4,5},{5,4},{6,7},{7,6},{8,9},{9,8},{10,11... | collective-permute-start | bytes 18440 | tf_op jit(solution)/shard_map/ppermute | solution.py:27
  41.7 4.2 %collective-permute-start.10 = (f32[8,512]{1,0:T(8,128)S(1)}, f32[8,512]{1,0:T(8,128)S(1)}, u32[]{:S(2)}, u32[]{:S(2)}) collective-permute-start(f32[8,512]{1,0:T(8,128)S(1)} %columns.2), channel_id=1, source_target_pairs={{0,6},{1,7},{2,4},{3,5},{4,2},{5,3},{6,0},{7,1},{8,14},{9,15},{10,... | collective-permute-start | bytes 49160 | tf_op jit(solution)/shard_map/ppermute | solution.py:27
  41.8 4.1 %collective-permute-start.8 = (f32[8,512]{1,0:T(8,128)S(1)}, f32[8,512]{1,0:T(8,128)S(1)}, u32[]{:S(2)}, u32[]{:S(2)}) collective-permute-start(f32[8,512]{1,0:T(8,128)S(1)} %columns.2), channel_id=1, source_target_pairs={{0,4},{1,5},{2,6},{3,7},{4,0},{5,1},{6,2},{7,3},{8,12},{9,13},{10,... | collective-permute-start | bytes 49160 | tf_op jit(solution)/shard_map/ppermute | solution.py:27
  42.7 3.5 %collective-permute-start.9 = (f32[8,512]{1,0:T(8,128)S(1)}, f32[8,512]{1,0:T(8,128)S(1)}, u32[]{:S(2)}, u32[]{:S(2)}) collective-permute-start(f32[8,512]{1,0:T(8,128)S(1)} %columns.2), channel_id=1, source_target_pairs={{0,2},{1,3},{2,0},{3,1},{4,6},{5,7},{6,4},{7,5},{8,10},{9,11},{10,... | collective-permute-start | bytes 49160 | tf_op jit(solution)/shard_map/ppermute | solution.py:27
  46.2 10.8 %collective-permute-start.11 = (f32[6,512]{1,0:T(8,128)S(1)}, f32[6,512]{1,0:T(8,128)S(1)}, u32[]{:S(2)}, u32[]{:S(2)}) collective-permute-start(f32[6,512]{1,0:T(8,128)S(1)} %slice_select_fusion), channel_id=1, source_target_pairs={{0,8},{1,9},{2,10},{3,11},{4,255},{5,254},{6,253},{7,252},{8,16},{... | collective-permute-start | bytes 36872 | tf_op jit(solution)/shard_map/ppermute | solution.py:27
  52.7 4.3 %collective-permute-start.12 = (f32[4,512]{1,0:T(4,128)S(1)}, f32[4,512]{1,0:T(4,128)S(1)}, u32[]{:S(2)}, u32[]{:S(2)}) collective-permute-start(f32[4,512]{1,0:T(4,128)S(1)} %slice_select_fusion.1), channel_id=1, source_target_pairs={{0,16},{1,17},{2,18},{3,19},{4,247},{5,246},{6,245},{7,244},{8,24}... | collective-permute-start | bytes 24584 | tf_op jit(solution)/shard_map/ppermute | solution.py:27
  52.7 4.0 %collective-permute-start.13 = (f32[2,512]{1,0:T(2,128)S(1)}, f32[2,512]{1,0:T(2,128)S(1)}, u32[]{:S(2)}, u32[]{:S(2)}) collective-permute-start(f32[2,512]{1,0:T(2,128)S(1)} %slice_select_fusion.3), channel_id=1, source_target_pairs={{0,24},{1,25},{2,26},{3,27},{4,239},{5,238},{6,237},{7,236},{8,35}... | collective-permute-start | bytes 12296 | tf_op jit(solution)/shard_map/ppermute | solution.py:27
  57.1 2.3 %collective-permute-start.14 = (f32[8,512]{1,0:T(8,128)S(1)}, f32[8,512]{1,0:T(8,128)S(1)}, u32[]{:S(2)}, u32[]{:S(2)}) collective-permute-start(f32[8,512]{1,0:T(8,128)S(1)} %multiply_add_fusion.2), channel_id=1, source_target_pairs={{0,4},{1,5},{2,6},{3,7},{4,0},{5,1},{6,2},{7,3},{8,12},{9,13},{10,... | collective-permute-start | bytes 49160 | tf_op jit(solution)/shard_map/ppermute | solution.py:27
  62.8 4.6 %collective-permute-start.15 = (f32[1024]{0:T(1024)S(1)}, f32[1024]{0:T(1024)S(1)}, u32[]{:S(2)}, u32[]{:S(2)}) collective-permute-start(f32[1024]{0:T(1024)S(1)} %bitcast.54), channel_id=1, source_target_pairs={{0,1},{1,0},{2,3},{3,2},{4,5},{5,4},{6,7},{7,6},{8,9},{9,8},{10,11... | collective-permute-start | bytes 12296 | tf_op jit(solution)/shard_map/ppermute | solution.py:27
  67.4 6.4 %copy-start.2 = (bf16[1024,256]{1,0:T(8,128)(2,1)S(1)}, bf16[1024,256]{1,0:T(8,128)(2,1)}, u32[]{:S(2)}) copy-start(bf16[1024,256]{1,0:T(8,128)(2,1)} %param.11) | copy-start | bytes 1572868
  70.6 3.4 %collective-permute-start.16 = (f32[8,512]{1,0:T(8,128)S(1)}, f32[8,512]{1,0:T(8,128)S(1)}, u32[]{:S(2)}, u32[]{:S(2)}) collective-permute-start(f32[8,512]{1,0:T(8,128)S(1)} %columns.3), channel_id=1, source_target_pairs={{0,4},{1,5},{2,6},{3,7},{4,0},{5,1},{6,2},{7,3},{8,12},{9,13},{10,... | collective-permute-start | bytes 49160 | tf_op jit(solution)/shard_map/ppermute | solution.py:27
  70.7 3.6 %collective-permute-start.17 = (f32[8,512]{1,0:T(8,128)S(1)}, f32[8,512]{1,0:T(8,128)S(1)}, u32[]{:S(2)}, u32[]{:S(2)}) collective-permute-start(f32[8,512]{1,0:T(8,128)S(1)} %columns.3), channel_id=1, source_target_pairs={{0,2},{1,3},{2,0},{3,1},{4,6},{5,7},{6,4},{7,5},{8,10},{9,11},{10,... | collective-permute-start | bytes 49160 | tf_op jit(solution)/shard_map/ppermute | solution.py:27
  72.7 4.6 %collective-permute-start.18 = (f32[8,512]{1,0:T(8,128)S(1)}, f32[8,512]{1,0:T(8,128)S(1)}, u32[]{:S(2)}, u32[]{:S(2)}) collective-permute-start(f32[8,512]{1,0:T(8,128)S(1)} %columns.3), channel_id=1, source_target_pairs={{0,6},{1,7},{2,4},{3,5},{4,2},{5,3},{6,0},{7,1},{8,14},{9,15},{10,... | collective-permute-start | bytes 49160 | tf_op jit(solution)/shard_map/ppermute | solution.py:27
  77.4 6.4 %collective-permute-start.20 = (f32[512]{0:T(512)S(1)}, f32[512]{0:T(512)S(1)}, u32[]{:S(2)}, u32[]{:S(2)}) collective-permute-start(f32[512]{0:T(512)S(1)} %bitcast.71), channel_id=1, source_target_pairs={{0,16},{1,17},{2,18},{3,19},{4,247},{5,246},{6,245},{7,244},{8,24}... | collective-permute-start | bytes 6152 | tf_op jit(solution)/shard_map/ppermute | solution.py:27
  81.7 2.8 %collective-permute-start.19 = (f32[2,512]{1,0:T(2,128)S(1)}, f32[2,512]{1,0:T(2,128)S(1)}, u32[]{:S(2)}, u32[]{:S(2)}) collective-permute-start(f32[2,512]{1,0:T(2,128)S(1)} %slice_select_fusion.2), channel_id=1, source_target_pairs={{0,8},{1,9},{2,10},{3,11},{4,255},{5,254},{6,253},{7,252},{8,16},{... | collective-permute-start | bytes 12296 | tf_op jit(solution)/shard_map/ppermute | solution.py:27
  84.5 5.8 %collective-permute-start.21 = (f32[2,512]{1,0:T(2,128)S(1)}, f32[2,512]{1,0:T(2,128)S(1)}, u32[]{:S(2)}, u32[]{:S(2)}) collective-permute-start(f32[2,512]{1,0:T(2,128)S(1)} %multiply_add_fusion.5), channel_id=1, source_target_pairs={{0,4},{1,5},{2,6},{3,7},{4,0},{5,1},{6,2},{7,3},{8,12},{9,13},{10,... | collective-permute-start | bytes 12296 | tf_op jit(solution)/shard_map/ppermute | solution.py:27
  90.3 2.8 %collective-permute-start.22 = (f32[512]{0:T(512)S(1)}, f32[512]{0:T(512)S(1)}, u32[]{:S(2)}, u32[]{:S(2)}) collective-permute-start(f32[512]{0:T(512)S(1)} %bitcast.66), channel_id=1, source_target_pairs={{0,1},{1,0},{2,3},{3,2},{4,5},{5,4},{6,7},{7,6},{8,9},{9,8},{10,11... | collective-permute-start | bytes 6152 | tf_op jit(solution)/shard_map/ppermute | solution.py:27
